TPU v7x, 32 devices: a whole 2x2x4 slice. The times are simulated.
32 devices in a mesh: head: 4 (over x, core), blk: 8 (over z, y).
Axes of the slice: x: 2, y: 2, z: 4, core: 2. Of those that a mesh axis runs over, the one named last changes fastest.
Arguments:
- tokens: bfloat16 [8192, 2048], P(('blk', 'head')), may hold values from -6 to 6
- doc_lengths: int32 [4], replicated, may hold values from 1 to 4096, 8192 in all
- norm1_gain: bfloat16 [2048], P(('head', 'blk')), may hold values from 0.25 to 1.75
- w_query: bfloat16 [2048, 1536], P(('head', 'blk')), may hold values from -0.125 to 0.125
- w_key: bfloat16 [2048, 384], P(('head', 'blk')), may hold values from -0.125 to 0.125
- w_value: bfloat16 [2048, 384], P(('head', 'blk')), may hold values from -0.125 to 0.125
- query_gain: bfloat16 [64], replicated, may hold values from 0.25 to 1.75
- key_gain: bfloat16 [64], replicated, may hold values from 0.25 to 1.75
- w_out: bfloat16 [1536, 2048], P(('head', 'blk')), may hold values from -1.25 to 1.25
- norm2_gain: bfloat16 [2048], P(('head', 'blk')), may hold values from 0.25 to 1.75
- w_gate: bfloat16 [2048, 5120], P(('head', 'blk')), may hold values from -0.125 to 0.125
- w_up: bfloat16 [2048, 5120], P(('head', 'blk')), may hold values from -0.125 to 0.125
- w_down: bfloat16 [5120, 2048], P(('head', 'blk')), may hold values from -0.078125 to 0.078125
- cotangent: bfloat16 [8192, 2048], P(('blk', 'head')), may hold values from -6 to 6
Outputs:
- out_act: bfloat16 [8192, 2048], P(('blk', 'head'))
- d_tokens: float32 [8192, 2048], P(('blk', 'head'))
- d_norm1_gain: float32 [2048], P(('head', 'blk'))
- d_w_query: float32 [2048, 1536], P(('head', 'blk'))
- d_w_key: float32 [2048, 384], P(('head', 'blk'))
- d_w_value: float32 [2048, 384], P(('head', 'blk'))
- d_query_gain: float32 [64], replicated
- d_key_gain: float32 [64], replicated
- d_w_out: float32 [1536, 2048], P(('head', 'blk'))
- d_norm2_gain: float32 [2048], P(('head', 'blk'))
- d_w_gate: float32 [2048, 5120], P(('head', 'blk'))
- d_w_up: float32 [2048, 5120], P(('head', 'blk'))
- d_w_down: float32 [5120, 2048], P(('head', 'blk'))
Inputs may be any that keep to these rules, and one draw needn't show every extreme that they name: `doc_lengths`: the documents lie end to end in order from token 0; their lengths sum to 8192 and one is exactly 4096 long.
All inputs are finite; a program needn't handle non-finite values.
Results may differ from a plain program's by a relative error of at most 0.018.
Values may be sent and summed in bfloat16 or wider, within the bound.
A program may use at most 320 MiB of HBM per device.

v0:
```python
import functools
import math

import jax
import jax.numpy as jnp
from jax import lax
from jax.experimental import pallas as pl
from jax.experimental.pallas import tpu as pltpu
from jax.sharding import PartitionSpec as P

QHEADS = 24
KVHEADS = 6
HEAD = 64
MAXDOC = 4096

EPS = 1e-06
SCALE = 0.125
LOG2E = 1.4426950408889634
NEG = -1e30
TILE = 256
BACK = 4
BF = jnp.bfloat16
F32 = jnp.float32


def matmul(left_side, right_side):
    return jnp.dot(left_side, right_side, preferred_element_type=F32)


def matmul_tn(left_side, right_side):
    return lax.dot_general(
        left_side, right_side, (((0,), (0,)), ((), ())), preferred_element_type=F32
    )


def matmul_nt(left_side, right_side):
    return lax.dot_general(
        left_side, right_side, (((1,), (1,)), ((), ())), preferred_element_type=F32
    )


def swap(block, axis, bit):
    count = lax.axis_size(axis)
    return lax.ppermute(block, axis, [(i, i ^ bit) for i in range(count)])


def ring(block, step):
    count = lax.axis_size("blk")
    return lax.ppermute(block, "blk", [(i, (i + step) % count) for i in range(count)])


def put(full, part, index, axis=0):
    return lax.dynamic_update_index_in_dim(full, part, index, axis)


def take(full, index, axis=0):
    return lax.dynamic_index_in_dim(full, index, axis, keepdims=False)


def place_of():
    at = lax.axis_index("blk")
    return at // 2, at % 2, lax.axis_size("blk") // 2


class LineScatter:
    def __init__(self, chunk):
        self.place, _, self.line = place_of()
        self.chunk = chunk
        self.step = 1
        self.total = chunk((self.place - 1) % self.line)

    def send(self):
        self.total = ring(self.total.astype(BF), 2)
        return self.total

    def add(self):
        self.step += 1
        mine = self.chunk((self.place - self.step) % self.line)
        self.total = self.total.astype(F32) + mine.astype(F32)

    def ahead(self, steps):
        for _ in range(steps):
            self.send()
            self.add()


def gather_blk(part, axis=0):
    place, side, line = place_of()
    shape = part.shape[:axis] + (line, 2) + part.shape[axis:]
    full = jnp.zeros(shape, part.dtype)
    held = part

    def store(full, block, source, side):
        block = block.reshape(block.shape[:axis] + (1, 1) + block.shape[axis:])
        at = [0] * full.ndim
        at[axis], at[axis + 1] = source, side
        return lax.dynamic_update_slice(full, block, at)

    for step in range(line):
        if step:
            held = ring(held, 2)
        other = swap(held, "blk", 1)
        source = (place - step) % line
        full = store(full, held, source, side)
        full = store(full, other, source, 1 - side)
    return full


def sync(*trees):
    return lax.optimization_barrier(trees)


def nt(left_side, right_side):
    return lax.dot_general(
        left_side, right_side, (((1,), (1,)), ((), ())), preferred_element_type=F32
    )


def nn(left_side, right_side):
    return lax.dot_general(
        left_side, right_side, (((1,), (0,)), ((), ())), preferred_element_type=F32
    )


def lanes(shape):
    return lax.broadcasted_iota(jnp.int32, shape, len(shape) - 1)


def transposed(block):
    return jnp.swapaxes(block, 0, 1)


def head_groups(meta_ref):
    odd = meta_ref[0]
    return ((4, 2 * odd, odd), (2, 4 * (1 - odd), 1 - odd))


def split_window(kv_ref, keys, values, step, slot):
    per_block = kv_ref.shape[2] // TILE
    block, part = step // per_block, step % per_block
    source = pl.ds(pl.multiple_of(part * TILE, TILE), TILE)
    target = pl.ds(pl.multiple_of(step * TILE, TILE), TILE)
    low = lanes((TILE, 128)) < HEAD
    both = kv_ref[block, slot, source, :].astype(F32)
    moved = pltpu.roll(both, HEAD, 1)
    keys[target, 0:128] = jnp.where(low, both, moved).astype(BF)
    values[target, :] = jnp.where(low, moved, 1.0).astype(BF)
    return target


def attend_kernel(
    meta_ref, query_ref, kv_ref, start_ref, out_ref, low_ref, acc_ref, keys, values
):
    heads, rows, _ = query_ref.shape
    base = keys.shape[1] - rows
    lane = lanes((TILE, 128))

    def fill(step, carry):
        for slot in range(2):
            split_window(kv_ref, keys.at[slot], values.at[slot], step, slot)
        return carry

    lax.fori_loop(0, keys.shape[1] // TILE, fill, 0)
    for count, first, slot in head_groups(meta_ref):
        for tile in range(rows // TILE):
            q_at = tile * TILE
            low, high = meta_ref[1 + 2 * tile], meta_ref[2 + 2 * tile]
            queries = query_ref[pl.ds(first, count), q_at : q_at + TILE, :].reshape(
                count * TILE, 2 * HEAD
            )
            acc = acc_ref.at[pl.ds(0, count * TILE)]
            acc[...] = jnp.zeros((count * TILE, 2 * HEAD), F32)
            start_col = start_ref[q_at : q_at + TILE, :]
            q_pos = base + q_at + lax.broadcasted_iota(jnp.int32, (TILE, 1), 0)

            def step(at, carry, masked, size=TILE):
                k_at = pl.multiple_of(at * TILE, TILE)
                scores = nt(queries, keys[slot, pl.ds(k_at, size), :])
                if masked:
                    k_pos = k_at + lax.broadcasted_iota(jnp.int32, (1, TILE), 1)
                    allowed = (start_col <= k_pos) & (k_pos <= q_pos)
                    scores = jnp.where(
                        allowed[None], scores.reshape(count, TILE, TILE), NEG
                    ).reshape(count * TILE, TILE)
                weights = jnp.exp2(scores).astype(BF)
                acc[...] += nn(weights, values[slot, pl.ds(k_at, size), :])
                return carry

            begin = low // TILE
            last = (base + q_at) // TILE
            clear = jnp.minimum((high + TILE - 1) // TILE, last)
            lax.fori_loop(begin, clear, functools.partial(step, masked=True), 0)
            pairs = (last - clear) // 4

            def wide_step(i, carry):
                return step(clear + 4 * i, carry, False, 4 * TILE)

            lax.fori_loop(0, pairs, wide_step, 0)
            lax.fori_loop(
                clear + 4 * pairs, last, functools.partial(step, masked=False), 0
            )
            step(last, 0, True)
            for j in range(count):
                part = acc_ref[j * TILE : (j + 1) * TILE, :]
                total = part[:, HEAD : HEAD + 1]
                out_ref[first + j, q_at : q_at + TILE, :] = jnp.where(
                    lane < HEAD, part / total, jnp.log2(total)
                )

    def lay(step, carry):
        tile = pl.ds(pl.multiple_of(step * TILE, TILE), TILE)
        for t in range(heads // 2):
            pair = jnp.where(
                lane < HEAD, out_ref[2 * t, tile, :], pltpu.roll(out_ref[2 * t + 1, tile, :], HEAD, 1)
            )
            low_ref[tile, t * 128 : (t + 1) * 128] = pair.astype(BF)
        return carry

    lax.fori_loop(0, rows // TILE, lay, 0)


def attend(meta, queries, kv, starts):
    heads, rows, _ = queries.shape
    window = kv.shape[0] * rows
    vmem = pl.BlockSpec(memory_space=pltpu.VMEM)
    return pl.pallas_call(
        attend_kernel,
        out_shape=(
            jax.ShapeDtypeStruct((heads, rows, 2 * HEAD), F32),
            jax.ShapeDtypeStruct((rows, heads * HEAD), BF),
        ),
        in_specs=[pl.BlockSpec(memory_space=pltpu.SMEM)] + [vmem] * 3,
        out_specs=(vmem, vmem),
        scratch_shapes=[
            pltpu.VMEM((4 * TILE, 2 * HEAD), F32),
            pltpu.VMEM((2, window, 2 * HEAD), BF),
            pltpu.VMEM((2, window, 2 * HEAD), BF),
        ],
        compiler_params=pltpu.CompilerParams(vmem_limit_bytes=48 << 20),
        cost_estimate=pl.CostEstimate(
            flops=60_000_000_000, bytes_accessed=20_000_000, transcendentals=20_000_000
        ),
        name="attend",
    )(meta, queries, kv, starts)


def attend_back_kernel(
    which,
    meta_ref,
    wide_ref,
    query_ref,
    kv_ref,
    out_ref,
    grad_ref,
    start_ref,
    dq_ref,
    low_ref,
    own_ref,
    keys,
    values,
    keys_t,
    query_t,
    grad_t,
    grads,
    dq,
    dkv,
):
    rows = query_ref.shape[1]
    window = keys.shape[0]
    base = window - rows
    lane = lanes((TILE, 128))
    low_lane = lane < HEAD
    count, first, slot = head_groups(meta_ref)[which]

    def fill(step, carry):
        target = split_window(kv_ref, keys, values, step, slot)
        keys[target, 128:256] = jnp.ones((TILE, 128), BF)
        keys_t[:, target] = transposed(keys[target, 0:128])[0:HEAD, :]
        dkv[target, :] = jnp.zeros((TILE, 128), F32)
        return carry

    lax.fori_loop(0, window // TILE, fill, 0)

    def low_terms(value, first):
        out = jnp.zeros_like(value)
        for i in range(3):
            term = value.astype(BF).astype(F32)
            out = jnp.where(lane == first + i, term, out)
            value = value - term
        return out

    def turn(step, carry):
        tile = pl.ds(pl.multiple_of(step * TILE, TILE), TILE)
        for j in range(count):
            query_t[j, 0:128, tile] = transposed(wide_ref[first + j, tile, :])
            kept = out_ref[first + j, tile, :]
            query_t[j, 128:256, tile] = transposed(low_terms(-kept, HEAD).astype(BF))
            pair = pl.ds(pl.multiple_of((first // 2 + j // 2) * 128, 128), 128)
            grad = grad_ref[tile, pair].astype(F32)
            moved = pltpu.roll(grad, HEAD, 1)
            if j % 2:
                grad, moved = moved, grad
            dots = jnp.sum(jnp.where(low_lane, grad * kept, 0.0), axis=1, keepdims=True)
            dots = jnp.broadcast_to(-dots, (TILE, 128))
            block = jnp.where(low_lane, grad, low_terms(dots, HEAD))
            grad_t[j, :, tile] = transposed(block.astype(BF))
            grads[j, tile, :] = jnp.where(low_lane, 0.0, moved).astype(BF)
            dq[j, :, tile] = jnp.zeros((HEAD, TILE), F32)
        return carry

    lax.fori_loop(0, rows // TILE, turn, 0)
    for tile in range(rows // TILE):
        q_at = tile * TILE
        q_cols = slice(q_at, q_at + TILE)
        low, high = meta_ref[1 + 2 * tile], meta_ref[2 + 2 * tile]
        start_row = start_ref[:, q_cols]
        q_pos = base + q_at + lax.broadcasted_iota(jnp.int32, (1, TILE), 1)

        def step(at, carry, masked, size=TILE):
            k_at = pl.multiple_of(at * TILE, TILE)
            k_rows = pl.ds(k_at, size)
            key_block = keys[k_rows, :]
            value_block = values[k_rows, :]
            key_t = keys_t[:, k_rows]
            if masked:
                k_pos = k_at + lax.broadcasted_iota(jnp.int32, (TILE, 1), 0)
                allowed = (start_row <= k_pos) & (k_pos <= q_pos)
            total = dkv[k_rows, :]
            for j in range(count):
                scores = nn(key_block, query_t[j, :, q_cols])
                if masked:
                    scores = jnp.where(allowed, scores, NEG)
                probs = jnp.exp2(scores)
                diff = nn(value_block, grad_t[j, :, q_cols])
                grad_score = (probs * diff).astype(BF)
                total = (
                    total
                    + nn(probs.astype(BF), grads[j, q_cols, :])
                    + nn(grad_score, query_ref[first + j, q_cols, :])
                )
                dq[j, :, q_cols] += nn(key_t, grad_score)
            dkv[k_rows, :] = total
            return carry

        begin = low // TILE
        last = (base + q_at) // TILE
        clear = jnp.minimum((high + TILE - 1) // TILE, last)
        lax.fori_loop(begin, clear, functools.partial(step, masked=True), 0)
        pairs = (last - clear) // 4

        def wide_step(i, carry):
            return step(clear + 4 * i, carry, False, 4 * TILE)

        lax.fori_loop(0, pairs, wide_step, 0)
        lax.fori_loop(
            clear + 4 * pairs, last, functools.partial(step, masked=False), 0
        )
        step(last, 0, True)

    def finish(step, carry):
        tile = pl.ds(pl.multiple_of(step * TILE, TILE), TILE)
        for t in range(count // 2):
            pair = jnp.concatenate([dq[2 * t, :, tile], dq[2 * t + 1, :, tile]], axis=0)
            dq_ref[tile, t * 128 : (t + 1) * 128] = transposed(pair) * SCALE
        for block in range(BACK + 1):
            source = pl.ds(pl.multiple_of(block * rows + step * TILE, TILE), TILE)
            part = dkv[source, :]
            part = jnp.where(low_lane, part * SCALE, part)
            if block < BACK:
                low_ref[(0, 2, 1, 3)[block], tile, :] = part.astype(BF)
            else:
                own_ref[tile, :] = part
        return carry

    lax.fori_loop(0, rows // TILE, finish, 0)


def attend_back(which, meta, wide, queries, kv, kept, grads, starts):
    _, rows, _ = queries.shape
    window = kv.shape[0] * rows
    count = (4, 2)[which]
    vmem = pl.BlockSpec(memory_space=pltpu.VMEM)
    shape = jax.ShapeDtypeStruct
    return pl.pallas_call(
        functools.partial(attend_back_kernel, which),
        out_shape=(
            shape((rows, count * HEAD), F32),
            shape((BACK, rows, 128), BF),
            shape((rows, 128), F32),
        ),
        in_specs=[pl.BlockSpec(memory_space=pltpu.SMEM)] + [vmem] * 6,
        out_specs=(vmem,) * 3,
        scratch_shapes=[
            pltpu.VMEM((window, 256), BF),
            pltpu.VMEM((window, 128), BF),
            pltpu.VMEM((HEAD, window), BF),
            pltpu.VMEM((count, 256, rows), BF),
            pltpu.VMEM((count, 128, rows), BF),
            pltpu.VMEM((count, rows, 128), BF),
            pltpu.VMEM((count, HEAD, rows), F32),
            pltpu.VMEM((window, 128), F32),
        ],
        compiler_params=pltpu.CompilerParams(vmem_limit_bytes=48 << 20),
        cost_estimate=pl.CostEstimate(
            flops=count * 20_000_000_000, bytes_accessed=40_000_000, transcendentals=20_000_000
        ),
        name=("attend_back_four", "attend_back_two")[which],
    )(meta, wide, queries, kv, kept, grads, starts)


MESH = pl.DeviceIdType.MESH
HEADS_OUT, SLAB, NEAR, FAR, ACROSS, FAR_ON, ACROSS_ON = 0, 3, 7, 8, 9, 10, 11
CORNER_TOP, CORNER_LOW, CORNER_ON, TO_MATE = 12, 13, 14, 15
BACK_TOP, BACK_LOW, BACK_FAR, BACK_ACROSS, HEADS_BACK, SUM_ON = 19, 20, 21, 22, 23, 26
WEIGHT_ON, TOP_ON, OUT_MATE, DOWN_LAST, WEIGHT_BACK, TRANSFERS = 30, 32, 36, 40, 41, 43
SPANS = ((0, 256), (256, 256), (512, 128))


def middle_kernel(
    slabs,
    downs,
    line,
    attn_ref,
    tokens_ref,
    w_own_ref,
    w_far_ref,
    gain_ref,
    top_ref,
    top_far_ref,
    top_across_ref,
    top_corner_ref,
    *refs,
):
    slab_refs, down_refs = refs[:slabs], refs[slabs : slabs + downs]
    (
        resid_out,
        grad_out,
        grad_low_out,
        mixed_out,
        heads_out,
        part_out,
        part_in,
        w_out_ref,
        gu_out,
        gu_next,
        down_out,
        weight_own,
        weight_in,
        sum_own,
        sum_far,
        sum_across,
        sum_corner,
        gain_out,
        mixed,
        acts,
        tops,
        w_gu,
        w_dn,
        hidden,
        grad_gu,
        pairs,
        got,
        stage,
        in_far,
        in_across,
        in_top,
        in_low,
        resid,
        turned,
        gu_stage,
        sends,
        recvs,
        locals_,
    ) = refs[slabs + downs :]
    me, at = lax.axis_index("head"), lax.axis_index("blk")
    count = lax.axis_size("blk")
    side, place = at % 2, at // 2
    odd = me % 2
    mate, beside, corner = me + 1 - 2 * odd, (me + 2) % 4, (me + 3 - 2 * odd) % 4
    other = at + 1 - 2 * side
    after, before = (at + 2) % count, (at + count - 2) % count
    rows, width = tokens_ref.shape
    half = rows // 2
    cols = mixed.shape[1] // 4
    units = w_dn.shape[0]
    slab_rows = slab_refs[0].shape[1]

    barrier = pltpu.get_barrier_semaphore()
    peers = ((mate, at), (beside, at), (corner, at), (me, other), (me, after), (me, before))
    for peer in peers:
        pl.semaphore_signal(barrier, inc=1, device_id=peer, device_id_type=MESH)
    pl.semaphore_wait(barrier, len(peers))

    def remote(index, source, target, device):
        return pltpu.make_async_remote_copy(
            src_ref=source,
            dst_ref=target,
            send_sem=sends.at[index],
            recv_sem=recvs.at[index],
            device_id=device,
            device_id_type=MESH,
        )

    def local(index, source, target):
        return pltpu.make_async_copy(source, target, locals_.at[index])

    def mixed_cols(head):
        return mixed.at[:, pl.ds(pl.multiple_of(head * cols, 128), cols)]

    heads = [
        remote(HEADS_OUT + i, attn_ref.at[to], mixed_cols(me), (to, at))
        for i, to in enumerate((mate, beside, corner))
    ]
    for copy in heads:
        copy.start()
    own_heads = local(0, attn_ref.at[me], mixed_cols(me))
    own_heads.start()

    def w_rows_of(head):
        return pairs.at[pl.ds(pl.multiple_of(head * cols, 128), cols)]

    weight_on = [
        remote(WEIGHT_ON, w_own_ref, w_rows_of(me), (mate, at)),
        remote(WEIGHT_ON + 1, w_far_ref, w_rows_of(beside), (mate, at)),
    ]
    for copy in weight_on:
        copy.start()
    load_out = [
        local(1, w_own_ref, w_rows_of(me)),
        local(2, w_far_ref, w_rows_of(beside)),
    ]
    for copy in load_out:
        copy.start()

    def slab_at(head, source):
        start = pl.multiple_of((head * line + source) * slab_rows, 16)
        return w_gu.at[pl.ds(start, slab_rows)]

    last = (place + line - (slabs - 1)) % line
    slab_on = [
        remote(SLAB + h, slab_refs[-1].at[h], slab_at(h, last), (me, after)) for h in range(4)
    ]
    for copy in slab_on:
        copy.start()
    load_slabs = [
        local(7 + 4 * i + h, ref.at[h], slab_at(h, (place + line - i) % line))
        for i, ref in enumerate(slab_refs)
        for h in range(4)
    ]
    for copy in load_slabs:
        copy.start()
    base_sem = 14 + 4 * slabs + downs
    if downs == 1:
        load_down = [local(14 + 4 * slabs, down_refs[0], w_dn)]
        down_last = []
    else:
        part_rows = units // line

        def down_at(source):
            return w_dn.at[pl.ds(pl.multiple_of(source * part_rows, 16), part_rows)]

        load_down = [
            local(14 + 4 * slabs + i, ref, down_at((place + line - i) % line))
            for i, ref in enumerate(down_refs)
        ]
        down_last = [remote(DOWN_LAST, down_refs[-1], down_at(last), (me, after))]
    for copy in down_last:
        copy.start()
    slot = side * 4 + me
    far_slot, across_slot = side * 4 + beside, (1 - side) * 4 + me
    corner_slot = (1 - side) * 4 + beside
    top_parts = (
        (top_ref, tops.at[slot]),
        (top_far_ref, tops.at[far_slot]),
        (top_across_ref, tops.at[across_slot]),
        (top_corner_ref, tops.at[corner_slot]),
    )
    load_top = [
        local(7 + 4 * slabs + i, source, target) for i, (source, target) in enumerate(top_parts)
    ]
    for copy in load_down + load_top:
        copy.start()

    for copy in heads + weight_on:
        copy.wait_recv()
    own_heads.wait()
    for copy in load_out:
        copy.wait()
    top_on = [
        remote(TOP_ON + i, source, target, (mate, at))
        for i, (source, target) in enumerate(top_parts)
    ]
    for copy in top_on:
        copy.start()
    keep_weight = local(base_sem, pairs.at[pl.ds(0, 4 * cols)], w_out_ref)
    keep_weight.start()
    keep_mixed = local(base_sem + 2, mixed, mixed_out)
    keep_mixed.start()

    def resid_cols(step, carry):
        span = pl.ds(pl.multiple_of(step * 256, 256), 256)
        weight = pairs[0 : 4 * cols, span]
        resid[:, span] = tokens_ref[:, span].astype(F32) + nn(mixed[...], weight)
        return carry

    lax.fori_loop(0, width // 256, resid_cols, 0)

    def norm_tile(step, carry):
        tile = pl.ds(pl.multiple_of(step * 32, 32), 32)
        block = resid[tile, :]
        scale = lax.rsqrt(jnp.mean(block * block, axis=1, keepdims=True) + EPS)
        acts[slot, tile, :] = (block * scale * gain_ref[...]).astype(BF)
        return carry

    lax.fori_loop(0, rows // 32, norm_tile, 0)
    keep_resid = local(base_sem + 3, resid, resid_out)
    keep_resid.start()

    near = remote(NEAR, acts.at[slot], acts.at[slot], (mate, at))
    far = remote(FAR, acts.at[slot], acts.at[slot], (beside, at))
    across = remote(ACROSS, acts.at[slot], acts.at[slot], (me, other))
    far_on = remote(FAR_ON, acts.at[far_slot], acts.at[far_slot], (mate, at))
    across_on = remote(ACROSS_ON, acts.at[across_slot], acts.at[across_slot], (mate, at))
    corner_on = remote(CORNER_ON, acts.at[corner_slot], acts.at[corner_slot], (mate, at))
    far_top = acts.at[far_slot, pl.ds(0, half)]
    across_low = acts.at[across_slot, pl.ds(half, half)]
    corner_top = remote(CORNER_TOP, far_top, far_top, (me, other))
    corner_low = remote(CORNER_LOW, across_low, across_low, (beside, at))
    near.start()
    far.start()
    across.start()
    far.wait_recv()
    far_on.start()
    corner_top.start()
    across.wait_recv()
    across_on.start()
    corner_low.start()
    for copy in load_slabs:
        copy.wait()
    for copy in slab_on + down_last:
        copy.wait_recv()
    for copy in load_down + load_top + [keep_weight]:
        copy.wait()
    for copy in top_on:
        copy.wait_recv()

    def pair_rows(index, first=0, size=rows):
        return pl.ds(pl.multiple_of(index * rows + first, 16), size)

    def to_mate(c):
        return remote(
            TO_MATE + c, pairs.at[pair_rows(2 * c + 1 - odd)], got.at[c], (mate, at)
        )

    def keep_part(c):
        return local(base_sem + 4, stage.at[odd], part_out.at[c])

    def part_on(c):
        return remote(OUT_MATE + c, stage.at[1 - odd], part_in.at[c], (mate, at))

    def chunk(c, carry):
        its_side = (side + c // 2) % 2
        its_head = (me + 2 * (c % 2)) % 4
        pair = its_side * 4 + its_head - its_head % 2

        @pl.when(c == 0)
        def _():
            near.wait_recv()

        @pl.when(c == 1)
        def _():
            far_on.wait_recv()

        @pl.when(c == 2)
        def _():
            corner_top.wait_recv()
            corner_low.wait_recv()
            corner_on.start()
            across_on.wait_recv()

        @pl.when(c == 3)
        def _():
            corner_on.wait_recv()

        for first, size in SPANS:
            block = acts[pl.ds(pair, 2)].reshape(2 * rows, width)
            gate = nn(block, w_gu[:, first : first + size])
            up = nn(block, w_gu[:, units + first : units + first + size])
            grad = nt(
                tops[pl.ds(pair, 2)].reshape(2 * rows, width), w_dn[first : first + size, :]
            )
            sig = jax.nn.sigmoid(gate)
            silu = gate * sig
            shape = (2, rows, size)
            hidden[pl.ds(pair, 2), :, first : first + size] = (
                (silu * up).astype(BF).reshape(shape)
            )
            grad_gu[pl.ds(pair, 2), :, first : first + size] = (
                (grad * up * sig * (1 + gate * (1 - sig))).astype(BF).reshape(shape)
            )
            grad_gu[pl.ds(pair, 2), :, units + first : units + first + size] = (
                (grad * silu).astype(BF).reshape(shape)
            )

        def grad_cols(step, carry):
            span = pl.ds(pl.multiple_of(step * 256, 256), 256)
            block = grad_gu[pl.ds(pair, 2)].reshape(2 * rows, 2 * units)
            part = nt(block, w_gu[span, :])
            pairs[pl.ds(pl.multiple_of(2 * c * rows, 128), 2 * rows), span] = part.astype(BF)
            return carry

        lax.fori_loop(0, width // 256, grad_cols, 0)
        to_mate(c).start()

        @pl.when(c > 0)
        def _():
            keep_part(c - 1).wait()
            part_on(c - 1).wait_send()

        def out_cols(step, carry):
            span = pl.ds(pl.multiple_of(step * 256, 256), 256)
            block = hidden[pl.ds(pair, 2)].reshape(2 * rows, units)
            part = nn(block, w_dn[:, span])
            stage[:, :, span] = part.astype(BF).reshape(2, rows, 256)
            return carry

        lax.fori_loop(0, width // 256, out_cols, 0)
        keep_part(c).start()
        part_on(c).start()
        return carry

    lax.fori_loop(0, 4, chunk, 0)

    def add_rows(c, first, extra):
        def tile(step, carry):
            span = pl.ds(pl.multiple_of(first + step * 32, 32), 32)
            mine = pair_rows(2 * c + odd, first + step * 32, 32)
            total = pairs[mine, :].astype(F32) + got[c, span, :].astype(F32)
            for ref in extra:
                total = total + ref[pl.ds(pl.multiple_of(step * 32, 32), 32), :].astype(F32)
            pairs[mine, :] = total.astype(BF)
            return carry

        lax.fori_loop(0, half // 32, tile, 0)

    back_top = remote(
        BACK_TOP, pairs.at[pair_rows(6 + odd, 0, half)], in_top, (me, other)
    )
    back_low = remote(
        BACK_LOW, pairs.at[pair_rows(6 + odd, half, half)], in_low, (beside, at)
    )
    back_far = remote(BACK_FAR, pairs.at[pair_rows(2 + odd)], in_far, (beside, at))
    back_across = remote(BACK_ACROSS, pairs.at[pair_rows(4 + odd)], in_across, (me, other))
    to_mate(3).wait_recv()
    add_rows(3, 0, ())
    back_top.start()
    add_rows(3, half, ())
    back_low.start()
    to_mate(1).wait_recv()
    to_mate(2).wait_recv()
    add_rows(1, half, ())
    add_rows(2, 0, ())

    keep_part(3).wait()
    part_on(3).wait_send()

    def gu_rows(step, carry):
        span = pl.ds(pl.multiple_of(step * 256, 256), 256)
        turned[...] = transposed(acts[:, :, span].reshape(8 * rows, 256))
        buffer = step % 2

        @pl.when(step > 1)
        def _():
            local(base_sem + 5 + buffer, gu_stage.at[buffer], gu_out.at[pl.ds(0, 256)]).wait()

        for n in range(2 * units // 256):
            part = nn(
                turned[...],
                grad_gu[:, :, n * 256 : (n + 1) * 256].reshape(8 * rows, 256),
            )
            gu_stage[buffer, :, n * 256 : (n + 1) * 256] = part.astype(BF)
        local(base_sem + 5 + buffer, gu_stage.at[buffer], gu_out.at[span]).start()
        return carry

    lax.fori_loop(0, 5, gu_rows, 0)
    back_top.wait_recv()
    add_rows(1, 0, (in_top,))
    back_far.start()
    back_low.wait_recv()
    add_rows(2, half, (in_low,))
    back_across.start()
    lax.fori_loop(5, width // 256, gu_rows, 0)
    for buffer in range(2):
        local(base_sem + 5 + buffer, gu_stage.at[buffer], gu_out.at[pl.ds(0, 256)]).wait()

    target = (place + line - 1) % line
    sum_on = [
        remote(
            SUM_ON + h,
            gu_out.at[pl.ds(pl.multiple_of((h * line + target) * slab_rows, 16), slab_rows)],
            gu_next.at[h],
            (me, after),
        )
        for h in range(4)
    ]
    for copy in sum_on:
        copy.start()

    for copy in (near, far, across, far_on, across_on, corner_on, corner_top, corner_low):
        copy.wait_send()
    load_again = [
        local(1 + i, w_out_ref.at[pl.ds(i * rows, rows)], acts.at[i]) for i in range(6)
    ]
    for copy in load_again:
        copy.start()

    for i, (first, size) in enumerate(SPANS):
        turned[0:size, :] = transposed(
            hidden[:, :, first : first + size].reshape(8 * rows, size)
        )
        buffer = i % 2
        if i > 1:
            local(base_sem + 7, stage.at[0], down_out.at[pl.ds(0, rows)]).wait()

        def down_cols(step, carry):
            span = pl.ds(pl.multiple_of(step * 256, 256), 256)
            part = nn(turned[0:size, :], tops[:, :, span].reshape(8 * rows, 256))
            stage[buffer, 0:size, span] = part.astype(BF)
            return carry

        lax.fori_loop(0, width // 256, down_cols, 0)
        local(
            base_sem + 7 + buffer,
            stage.at[buffer, pl.ds(0, size)],
            down_out.at[pl.ds(first, size)],
        ).start()

    to_mate(0).wait_recv()
    back_far.wait_recv()
    back_across.wait_recv()
    keep_resid.wait()
    gain_out[...] = jnp.zeros_like(gain_out)
    low = got.at[0]

    def norm_back(step, carry):
        tile = pl.ds(pl.multiple_of(step * 32, 32), 32)
        grad = (
            pairs[pair_rows(odd, step * 32, 32), :].astype(F32)
            + got[0, tile, :].astype(F32)
            + in_far[tile, :].astype(F32)
            + in_across[tile, :].astype(F32)
        )
        block = resid[tile, :]
        scale = lax.rsqrt(jnp.mean(block * block, axis=1, keepdims=True) + EPS)
        gain_out[...] += jnp.sum(grad * block * scale, axis=0, keepdims=True)
        inner = grad * gain_ref[...]
        mean = jnp.mean(inner * block, axis=1, keepdims=True)
        total = (
            tops[slot, tile, :].astype(F32)
            + scale * inner
            - block * (scale * scale * scale * mean)
        )
        resid[tile, :] = total
        low[tile, :] = total.astype(BF)
        return carry

    lax.fori_loop(0, rows // 32, norm_back, 0)
    keep_grad = local(base_sem + 3, resid, grad_out)
    keep_grad.start()
    keep_low = local(base_sem + 4, low, grad_low_out)
    keep_low.start()
    keep_mixed.wait()
    for copy in load_again:
        copy.wait()

    def heads_cols(step, carry):
        span = pl.ds(pl.multiple_of(step * 256, 256), 256)
        turned[:, span] = nt(low[...], acts[step]).astype(BF)
        return carry

    lax.fori_loop(0, 6, heads_cols, 0)

    def grad_cols_of(head):
        return turned.at[:, pl.ds(pl.multiple_of(head * cols, 128), cols)]

    heads_on = [
        remote(HEADS_BACK + i, grad_cols_of(to), heads_out.at[me], (to, at))
        for i, to in enumerate((mate, beside, corner))
    ]
    for copy in heads_on:
        copy.start()
    own_back = local(0, grad_cols_of(me), heads_out.at[me])
    own_back.start()

    for c in range(4):
        part_on(c).wait_recv()
    load_parts = [
        local(1, part_out, tops.at[pl.ds(0, 4)]),
        local(2, part_in, tops.at[pl.ds(4, 4)]),
    ]
    for copy in load_parts:
        copy.start()

    for c in range(4):
        to_mate(c).wait_send()
    for copy in (back_top, back_low, back_far, back_across):
        copy.wait_send()

    def weight_rows(step, carry):
        span = pl.ds(pl.multiple_of(step * 256, 256), 256)
        left = transposed(mixed[:, span])
        for n in range(width // 512):
            part = nn(left, low[:, n * 512 : (n + 1) * 512])
            pairs[span, n * 512 : (n + 1) * 512] = part.astype(BF)
        return carry

    lax.fori_loop(0, 6, weight_rows, 0)
    weight_back = [
        remote(WEIGHT_BACK, w_rows_of(mate), weight_in.at[0], (mate, at)),
        remote(WEIGHT_BACK + 1, w_rows_of(corner), weight_in.at[1], (mate, at)),
    ]
    keep_back = [
        local(3, w_rows_of(me), weight_own.at[0]),
        local(4, w_rows_of(beside), weight_own.at[1]),
    ]
    for copy in weight_back + keep_back:
        copy.start()
    for copy in load_parts:
        copy.wait()

    def add_out(step, carry):
        tile = pl.ds(pl.multiple_of(step % (rows // 32) * 32, 32), 32)
        c = step // (rows // 32)
        total = tops[c, tile, :].astype(F32) + tops[c + 4, tile, :].astype(F32)
        tops[c, tile, :] = total.astype(BF)
        return carry

    lax.fori_loop(0, 4 * rows // 32, add_out, 0)
    keep_sums = [
        local(7 + c, tops.at[c], ref)
        for c, ref in enumerate((sum_own, sum_far, sum_across, sum_corner))
    ]
    for copy in keep_sums:
        copy.start()
    for copy in weight_back + keep_back + keep_sums:
        copy.wait()

    own_back.wait()
    keep_grad.wait()
    keep_low.wait()
    local(base_sem + 7, stage.at[0, pl.ds(0, SPANS[2][1])], down_out.at[pl.ds(0, SPANS[2][1])]).wait()
    local(base_sem + 8, stage.at[1], down_out.at[pl.ds(0, rows)]).wait()
    for copy in heads_on + sum_on:
        copy.wait()
    for copy in heads + slab_on + down_last:
        copy.wait_send()
    for copy in weight_on + top_on:
        copy.wait_send()


def middle(attn_out, tokens, w_own, w_far, gain, tops, slabs, downs):
    rows, width = tokens.shape
    units = slabs[0].shape[2] // 2
    cols = attn_out.shape[2]
    line = lax.axis_size("blk") // 2
    slab_shape = slabs[0].shape
    anywhere = pl.BlockSpec(memory_space=pl.ANY)
    vmem = pl.BlockSpec(memory_space=pltpu.VMEM)
    shape = jax.ShapeDtypeStruct
    eight, four = (8, rows, width), (4, rows, width)
    return pl.pallas_call(
        functools.partial(middle_kernel, len(slabs), len(downs), line),
        out_shape=(
            shape((rows, width), F32),
            shape((rows, width), F32),
            shape((rows, width), BF),
            shape((rows, 4 * cols), BF),
            shape(attn_out.shape, BF),
            shape(four, BF),
            shape(four, BF),
            shape((4 * cols, width), BF),
            shape((width, 2 * units), BF),
            shape(slab_shape, BF),
            shape((units, width), BF),
            shape((2, cols, width), BF),
            shape((2, cols, width), BF),
            shape((rows, width), BF),
            shape((rows, width), BF),
            shape((rows, width), BF),
            shape((rows, width), BF),
            shape((1, width), F32),
        ),
        in_specs=[anywhere, vmem, anywhere, anywhere, vmem]
        + [anywhere] * (len(tops) + len(slabs) + len(downs)),
        out_specs=(anywhere,) * 17 + (vmem,),
        scratch_shapes=[
            pltpu.VMEM((rows, 4 * cols), BF),
            pltpu.VMEM(eight, BF),
            pltpu.VMEM(eight, BF),
            pltpu.VMEM((width, 2 * units), BF),
            pltpu.VMEM((units, width), BF),
            pltpu.VMEM((8, rows, units), BF),
            pltpu.VMEM((8, rows, 2 * units), BF),
            pltpu.VMEM((8 * rows, width), BF),
            pltpu.VMEM(four, BF),
            pltpu.VMEM((2, rows, width), BF),
            pltpu.VMEM((rows, width), BF),
            pltpu.VMEM((rows, width), BF),
            pltpu.VMEM((rows // 2, width), BF),
            pltpu.VMEM((rows // 2, width), BF),
            pltpu.VMEM((rows, width), F32),
            pltpu.VMEM((256, 8 * rows), BF),
            pltpu.VMEM((2, 256, 2 * units), BF),
            pltpu.SemaphoreType.DMA((TRANSFERS,)),
            pltpu.SemaphoreType.DMA((TRANSFERS,)),
            pltpu.SemaphoreType.DMA((24 + 4 * len(slabs) + len(downs),)),
        ],
        compiler_params=pltpu.CompilerParams(
            collective_id=1, has_side_effects=True, vmem_limit_bytes=60 << 20
        ),
        cost_estimate=pl.CostEstimate(
            flops=60_000_000_000, bytes_accessed=100_000_000, transcendentals=2_000_000
        ),
        name="middle",
    )(attn_out, tokens, w_own, w_far, gain, *tops, *slabs, *downs)


TOK_NEAR, TOK_FAR, TOK_ON, IN_QUERY, IN_REST = 0, 1, 2, 3, 6
TOP_FAR = 9
UNITS_MOVE, SLAB_ON, DOWN_ON = 11, 18, 19
KV_ONE, KV_TWO, KV_PAIR_ONE, KV_PAIR_TWO, FIRST_TRANSFERS = 20, 21, 22, 23, 24
COLS_Q = QHEADS // 4 * HEAD
COLS_IN = COLS_Q + 4 * HEAD


def head_scale(block):
    low = lanes(block.shape) < HEAD
    square = block * block
    first = jnp.sum(jnp.where(low, square, 0.0), axis=1, keepdims=True)
    second = jnp.sum(jnp.where(low, 0.0, square), axis=1, keepdims=True)
    return jnp.where(
        low, lax.rsqrt(first / HEAD + EPS), lax.rsqrt(second / HEAD + EPS)
    )


def swap_halves(block):
    low = lanes(block.shape) % HEAD < HEAD // 2
    return jnp.where(low, pltpu.roll(block, 96, 1), pltpu.roll(block, 32, 1))


def first_kernel(
    line,
    tokens_ref,
    query_ref,
    rest_ref,
    gate_ref,
    up_ref,
    down_ref,
    w_out_ref,
    top_ref,
    cos_ref,
    sin_ref,
    query_gain_ref,
    key_gain_ref,
    wide_out,
    query_out,
    kv_out,
    raw_out,
    normed_out,
    w_in_out,
    top_far_out,
    w_out_all,
    slab_out,
    slab_next,
    down_next,
    toks_out,
    gain_out,
    toks,
    normed,
    w_in,
    raw,
    wide,
    query,
    kv_own,
    gate,
    up,
    blocks,
    sends,
    recvs,
    ring_sends,
    ring_recvs,
    swap_sends,
    swap_recvs,
    out_ring_sends,
    out_ring_recvs,
    out_swap_sends,
    out_swap_recvs,
    locals_,
):
    me, at = lax.axis_index("head"), lax.axis_index("blk")
    count = lax.axis_size("blk")
    side, place = at % 2, at // 2
    odd = me % 2
    mate, beside, corner = me + 1 - 2 * odd, (me + 2) % 4, (me + 3 - 2 * odd) % 4
    other = at + 1 - 2 * side
    after, before = (at + 2) % count, (at + count - 2) % count
    rows, width = tokens_ref.shape
    half = rows // 2
    w_rows = query_ref.shape[0]
    units = slab_out.shape[2] // 2

    barrier = pltpu.get_barrier_semaphore()
    peers = [(mate, at), (beside, at), (corner, at), (me, after), (me, before)]
    peers += [(head, other) for head in (me, mate, beside, corner)]
    for peer in peers:
        pl.semaphore_signal(barrier, inc=1, device_id=peer, device_id_type=MESH)
    pl.semaphore_wait(barrier, len(peers))

    def remote(index, source, target, device, send=sends, recv=recvs):
        return pltpu.make_async_remote_copy(
            src_ref=source,
            dst_ref=target,
            send_sem=send.at[index],
            recv_sem=recv.at[index],
            device_id=device,
            device_id_type=MESH,
        )

    def local(index, source, target):
        return pltpu.make_async_copy(source, target, locals_.at[index])

    def cols_of(ref, start, size):
        return ref.at[:, pl.ds(pl.multiple_of(start, 128), size)]

    own_q = w_in.at[me, at, :, pl.ds(0, COLS_Q)]
    own_rest = w_in.at[me, at, :, pl.ds(COLS_Q, COLS_Q)]
    split = []
    for i, to in enumerate((mate, beside, corner)):
        split.append(
            remote(IN_QUERY + i, cols_of(query_ref, to * COLS_Q, COLS_Q), own_q, (to, at))
        )
        split.append(remote(IN_REST + i, rest_ref.at[to], own_rest, (to, at)))
    for copy in split:
        copy.start()
    own = [
        local(0, cols_of(query_ref, me * COLS_Q, COLS_Q), own_q),
        local(1, rest_ref.at[me], own_rest),
        local(2, tokens_ref, toks.at[me]),
        local(3, w_out_ref, w_out_all.at[at]),
    ]
    for copy in own:
        copy.start()
    tok_near = remote(TOK_NEAR, tokens_ref, toks.at[me], (mate, at))
    tok_far = remote(TOK_FAR, tokens_ref, toks.at[me], (beside, at))
    tok_on = remote(TOK_ON, toks.at[beside], toks.at[beside], (mate, at))
    tok_far.start()
    tok_near.start()
    down_on = remote(DOWN_ON, down_ref, down_next, (me, after))
    down_on.start()
    own_units = [local(4, gate_ref, gate), local(5, up_ref, up)]
    for copy in own_units:
        copy.start()

    def ring_copy(step):
        block = w_in.at[:, (at + count - 2 * (step - 1)) % count]
        return remote(step, block, block, (me, after), ring_sends, ring_recvs)

    def swap_copy(step):
        block = w_in.at[:, (at + count - 2 * step) % count]
        return remote(step, block, block, (me, other), swap_sends, swap_recvs)

    def out_ring(step):
        index = (at + count - 2 * (step - 1)) % count
        source = w_out_ref if step == 1 else w_out_all.at[index]
        return remote(
            step, source, w_out_all.at[index], (me, after), out_ring_sends, out_ring_recvs
        )

    def out_swap(step):
        index = (at + count - 2 * step) % count
        source = w_out_ref if step == 0 else w_out_all.at[index]
        return remote(
            step, source, w_out_all.at[index], (me, other), out_swap_sends, out_swap_recvs
        )

    out_ring(1).start()
    out_swap(0).start()

    for copy in own_units:
        copy.wait()
    ff_rows = units // line
    for j, ref in enumerate((gate, up)):
        for head in range(4):
            columns = ref[:, 2 * units * head : 2 * units * (head + 1)].astype(F32)
            for to_side in range(2):
                chosen = [
                    columns[:, (2 * z + to_side) * ff_rows : (2 * z + to_side + 1) * ff_rows]
                    for z in range(line)
                ]
                blocks[to_side, head, :, j * units : (j + 1) * units] = jnp.concatenate(
                    chosen, axis=1
                ).astype(BF)
    slab_rows = pl.ds(pl.multiple_of(side * w_rows, 16), w_rows)
    targets = [(side, mate), (side, beside), (side, corner)]
    targets += [(1 - side, head) for head in (me, mate, beside, corner)]
    spread = [
        remote(
            UNITS_MOVE + i,
            blocks.at[to_side, to_head],
            slab_out.at[me, slab_rows],
            (to_head, at if i < 3 else other),
        )
        for i, (to_side, to_head) in enumerate(targets)
    ]
    for copy in spread:
        copy.start()
    own_block = local(6, blocks.at[side, me], slab_out.at[me, slab_rows])
    own_block.start()
    for copy in split:
        copy.wait_recv()
    own[0].wait()
    own[1].wait()
    ring_copy(1).start()
    swap_copy(0).start()
    tok_far.wait_recv()
    tok_on.start()
    top_far = remote(TOP_FAR, top_ref, top_far_out, (beside, at))
    top_far.start()
    for step in range(1, line):
        ring_copy(step).wait_recv()
        if step < line - 1:
            ring_copy(step + 1).start()
        swap_copy(step).start()
        out_ring(step).wait_recv()
        if step < line - 1:
            out_ring(step + 1).start()

    for copy in spread:
        copy.wait_recv()
    own_block.wait()
    slab_on = remote(SLAB_ON, slab_out, slab_next, (me, after))
    slab_on.start()
    tok_near.wait_recv()
    tok_on.wait_recv()
    own[2].wait()
    own[3].wait()
    for step in range(line):
        swap_copy(step).wait_recv()
    for step in range(1, line):
        out_swap(step).start()
    keep_in = [
        local(7 + h, w_in.at[h], w_in_out.at[h]) for h in range(4)
    ]
    for copy in keep_in:
        copy.start()

    gains = w_in[:, :, :, COLS_IN : COLS_IN + 128].reshape(width, 128).astype(F32)
    gain_out[...] = transposed(gains)[0:8, :]

    def norm_tile(step, carry):
        head, tile = step // (rows // 32), pl.ds(pl.multiple_of(step % (rows // 32) * 32, 32), 32)
        block = toks[head, tile, :].astype(F32)
        scale = lax.rsqrt(jnp.mean(block * block, axis=1, keepdims=True) + EPS)
        normed[pl.ds(pl.multiple_of(step * 32, 32), 32), :] = (
            block * scale * gain_out[0:1, :]
        ).astype(BF)
        return carry

    lax.fori_loop(0, 4 * rows // 32, norm_tile, 0)
    keep_normed = local(11, normed, normed_out)
    keep_normed.start()
    keep_toks = local(16, toks, toks_out)
    keep_toks.start()

    def project(step, carry):
        tile = pl.ds(pl.multiple_of(step * 256, 256), 256)
        for first, size in SPANS:
            weight = w_in[:, :, :, first : first + size].reshape(width, size)
            raw[tile, first : first + size] = nn(normed[tile, :], weight)
        return carry

    lax.fori_loop(0, 4 * rows // 256, project, 0)
    keep_raw = local(12, raw.at[:, pl.ds(0, COLS_Q + 128)], raw_out)
    keep_raw.start()

    def rotated(block, gain, tile):
        block = block * head_scale(block) * gain
        return block * cos_ref[tile, :] + swap_halves(block) * sin_ref[tile, :]

    def prepare(step, carry):
        tile = pl.ds(pl.multiple_of(step * 64, 64), 64)
        first_half = lanes((64, 128)) < HEAD
        for t in range(QHEADS // 4 // 2):
            block = rotated(raw[tile, t * 128 : (t + 1) * 128], query_gain_ref[...], tile)
            block = block.astype(BF).astype(F32)
            moved = pltpu.roll(block, HEAD, 1)
            query[2 * t, tile, :] = jnp.where(first_half, block, 0.0).astype(BF)
            query[2 * t + 1, tile, :] = jnp.where(first_half, moved, 0.0).astype(BF)
            scaled = block * (SCALE * LOG2E)
            upper = scaled.astype(BF).astype(F32)
            lower = scaled - upper
            wide[2 * t, tile, :] = jnp.where(
                first_half, upper, pltpu.roll(lower, HEAD, 1)
            ).astype(BF)
            wide[2 * t + 1, tile, :] = jnp.where(
                first_half, pltpu.roll(upper, HEAD, 1), lower
            ).astype(BF)
        keys = rotated(raw[tile, COLS_Q : COLS_Q + 128], key_gain_ref[...], tile)
        values = raw[tile, COLS_Q + 128 : COLS_Q + 256]
        kv_own[0, tile, :] = jnp.where(
            first_half, keys, pltpu.roll(values, HEAD, 1)
        ).astype(BF)
        kv_own[1, tile, :] = jnp.where(
            first_half, pltpu.roll(keys, HEAD, 1), values
        ).astype(BF)
        return carry

    lax.fori_loop(0, 4 * rows // 64, prepare, 0)

    kv_one = remote(KV_ONE, kv_own, kv_out.at[2], (me, after))
    kv_two = remote(KV_TWO, kv_out.at[2], kv_out.at[0], (me, after))
    pair_one_even = remote(KV_PAIR_ONE, kv_own, kv_out.at[3], (me, other))
    pair_one_odd = remote(KV_PAIR_ONE, kv_out.at[2], kv_out.at[3], (me, other))
    pair_two_even = remote(KV_PAIR_TWO, kv_out.at[2], kv_out.at[1], (me, other))
    pair_two_odd = remote(KV_PAIR_TWO, kv_out.at[0], kv_out.at[1], (me, other))
    kv_one.start()

    @pl.when(side == 0)
    def _():
        pair_one_even.start()

    keep = [
        local(13, kv_own, kv_out.at[4]),
        local(14, wide, wide_out),
        local(15, query, query_out),
    ]
    for copy in keep:
        copy.start()
    kv_one.wait_recv()
    kv_two.start()

    @pl.when(side == 0)
    def _():
        pair_two_even.start()

    @pl.when(side == 1)
    def _():
        pair_one_odd.start()

    kv_two.wait_recv()

    @pl.when(side == 1)
    def _():
        pair_two_odd.start()

    pair_one_even.wait_recv()
    pair_two_even.wait_recv()
    down_on.wait_recv()
    slab_on.wait_recv()
    top_far.wait_recv()
    for copy in keep + keep_in + [keep_normed, keep_raw, keep_toks]:
        copy.wait()
    for copy in split + spread:
        copy.wait_send()
    for copy in (tok_near, tok_far, tok_on, top_far):
        copy.wait_send()
    for copy in (slab_on, down_on, kv_one, kv_two):
        copy.wait_send()
    pair_one_even.wait_send()
    pair_two_even.wait_send()

    for step in range(line):
        swap_copy(step).wait_send()
        out_swap(step).wait()
        if step:
            ring_copy(step).wait_send()
            out_ring(step).wait_send()


def first(
    tokens, w_query, rest, w_gate, w_up, w_down, w_out, cotangent, cosine, sine, query_gain, key_gain
):
    rows, width = tokens.shape
    count = lax.axis_size("blk")
    w_rows, ff = w_gate.shape
    units = ff // 8
    block = 4 * rows
    anywhere = pl.BlockSpec(memory_space=pl.ANY)
    vmem = pl.BlockSpec(memory_space=pltpu.VMEM)
    shape = jax.ShapeDtypeStruct
    heads = QHEADS // 4
    slab = shape((4, 2 * w_rows, 2 * units), BF)
    dma = pltpu.SemaphoreType.DMA
    return pl.pallas_call(
        functools.partial(first_kernel, count // 2),
        out_shape=(
            shape((heads, block, 128), BF),
            shape((heads, block, 128), BF),
            shape((BACK + 1, 2, block, 128), BF),
            shape((block, COLS_Q + 128), F32),
            shape((block, width), BF),
            shape((4, count, w_rows, 2 * COLS_Q), BF),
            shape((rows, width), BF),
            shape((count,) + w_out.shape, BF),
            slab,
            slab,
            shape(w_down.shape, BF),
            shape((4, rows, width), BF),
            shape((8, width), F32),
        ),
        in_specs=[anywhere] * 8 + [vmem] * 4,
        out_specs=(anywhere,) * 12 + (vmem,),
        scratch_shapes=[
            pltpu.VMEM((4, rows, width), BF),
            pltpu.VMEM((block, width), BF),
            pltpu.VMEM((4, count, w_rows, 2 * COLS_Q), BF),
            pltpu.VMEM((block, COLS_IN), F32),
            pltpu.VMEM((heads, block, 128), BF),
            pltpu.VMEM((heads, block, 128), BF),
            pltpu.VMEM((2, block, 128), BF),
            pltpu.VMEM(w_gate.shape, BF),
            pltpu.VMEM(w_up.shape, BF),
            pltpu.VMEM((2, 4, w_rows, 2 * units), BF),
            dma((FIRST_TRANSFERS,)),
            dma((FIRST_TRANSFERS,)),
            dma((count // 2,)),
            dma((count // 2,)),
            dma((count // 2,)),
            dma((count // 2,)),
            dma((count // 2,)),
            dma((count // 2,)),
            dma((count // 2,)),
            dma((count // 2,)),
            dma((17,)),
        ],
        compiler_params=pltpu.CompilerParams(
            collective_id=2, has_side_effects=True, vmem_limit_bytes=48 << 20
        ),
        cost_estimate=pl.CostEstimate(
            flops=60_000_000_000, bytes_accessed=60_000_000, transcendentals=1_000_000
        ),
        name="first",
    )(
        tokens, w_query, rest, w_gate, w_up, w_down, w_out, cotangent, cosine, sine,
        query_gain, key_gain,
    )


THREE, ONE, FOUR_ON, TWO_ON = 0, 2, 4, 6
UNITS_HOME, DOWN_STEP = 8, 15
PART_MATE, PART_CORNER, PART_FAR, QUERY_HOME, REST_HOME = 17, 18, 19, 20, 23
LAST_TRANSFERS = 26


def head_means(block):
    low = lanes(block.shape) < HEAD
    first = jnp.sum(jnp.where(low, block, 0.0), axis=1, keepdims=True)
    second = jnp.sum(jnp.where(low, 0.0, block), axis=1, keepdims=True)
    return jnp.where(low, first, second) * (1.0 / HEAD)


class LineSum:
    def __init__(self, part, got, hold, arrive, sems, places, remote):
        self.part, self.got, self.hold, self.arrive = part, got, hold, arrive
        self.swap_sems, self.ring_sems = sems
        self.side, self.place, self.line, self.other, self.after = places
        self.remote = remote

    def target(self, step):
        return (self.place + self.line - step) % self.line

    def swap(self, step):
        to = self.target(step)
        return self.remote(
            step - 1,
            self.part(2 * to + 1 - self.side),
            self.got.at[to],
            self.other,
            *self.swap_sems,
        )

    def pass_on(self, step):
        return self.remote(
            step - 1, self.hold.at[step - 1], self.arrive.at[step - 1], self.after, *self.ring_sems
        )

    def start(self):
        for step in range(1, self.line + 1):
            self.swap(step).start()

    def step(self, step, out=None):
        to = self.target(step)
        self.swap(step).wait_recv()
        total = self.part(2 * to + self.side)[...].astype(F32) + self.got[to].astype(F32)
        if step > 1:
            self.pass_on(step - 1).wait_recv()
            total = total + self.arrive[step - 2].astype(F32)
        if step < self.line:
            self.hold[step - 1] = total.astype(BF)
            self.pass_on(step).start()
        else:
            out[...] = total.astype(out.dtype)

    def drain(self):
        for step in range(1, self.line + 1):
            self.swap(step).wait_send()
            if step < self.line:
                self.pass_on(step).wait_send()


def last_kernel(
    line,
    dq_four_ref,
    dq_two_ref,
    low_four_ref,
    low_two_ref,
    own_four_ref,
    own_two_ref,
    pair_four_ref,
    raw_ref,
    cos_ref,
    sin_ref,
    query_gain_ref,
    key_gain_ref,
    normed_ref,
    w_in_ref,
    toks_ref,
    gain_ref,
    gain_two_ref,
    units_ref,
    units_parts_ref,
    down_ref,
    down_parts_ref,
    slab_ref,
    grad_ref,
    dx_out,
    query_out,
    key_out,
    value_out,
    norm_out,
    gate_out,
    up_out,
    down_out,
    w_out_out,
    gains_out,
    low,
    three,
    one,
    four_in,
    two_in,
    raw,
    normed,
    turned,
    w_in,
    toks,
    scales,
    grads,
    query_part,
    rest_part,
    query_got,
    rest_got,
    query_hold,
    rest_hold,
    query_arrive,
    rest_arrive,
    query_sum,
    rest_sum,
    slab,
    slab_got,
    slab_hold,
    slab_arrive,
    units_sum,
    units_in,
    query_in,
    rest_in,
    down_own,
    down_in,
    parts,
    part_got,
    part_far,
    gain_rows,
    head_gains,
    gains_in,
    sends,
    recvs,
    line_sems,
    gain_sends,
    gain_recvs,
    locals_,
):
    me, at = lax.axis_index("head"), lax.axis_index("blk")
    count = lax.axis_size("blk")
    side, place = at % 2, at // 2
    odd = me % 2
    mate, beside, corner = me + 1 - 2 * odd, (me + 2) % 4, (me + 3 - 2 * odd) % 4
    other = at + 1 - 2 * side
    after, before = (at + 2) % count, (at + count - 2) % count
    rows, width = dx_out.shape
    block = 4 * rows
    w_rows = w_in_ref.shape[2]

    rounds = [(mate, at), (beside, at), (me, other)]
    bit = 1
    while bit < line:
        rounds.append((me, at + 2 * bit * (1 - 2 * ((place // bit) % 2))))
        bit *= 2
    barrier = pltpu.get_barrier_semaphore()
    peers = [(corner, at), (me, after), (me, before)]
    peers += [(head, other) for head in (mate, beside, corner)] + rounds
    for peer in peers:
        pl.semaphore_signal(barrier, inc=1, device_id=peer, device_id_type=MESH)

    pl.semaphore_wait(barrier, len(peers))

    def remote(index, source, target, device, send=sends, recv=recvs):
        return pltpu.make_async_remote_copy(
            src_ref=source,
            dst_ref=target,
            send_sem=send.at[index],
            recv_sem=recv.at[index],
            device_id=device,
            device_id_type=MESH,
        )

    def local(index, source, target):
        return pltpu.make_async_copy(source, target, locals_.at[index])

    units_own_part = parts.at[:, pl.ds(0, 2 * w_rows), pl.ds(0, units_ref.shape[2])]
    low_refs, own_refs = (low_four_ref, low_two_ref), (own_four_ref, own_two_ref)
    three_on = remote(THREE, low_refs[1].at[2], three.at[1], (me, other))
    one_on = remote(ONE, low_refs[1].at[3], one.at[1], (me, other))
    three_on.start()
    one_on.start()
    low_loads = [local(6 + g, low_refs[g].at[pl.ds(0, 2)], low.at[g]) for g in (0, 1)]
    pair_loads = [
        local(11, pair_four_ref.at[0], three.at[0]),
        local(12, pair_four_ref.at[1], one.at[0]),
    ]
    for copy in low_loads + pair_loads:
        copy.start()
    loads = [
        local(0, normed_ref, normed),
        local(1, raw_ref, raw),
        local(2, w_in_ref, w_in),
        local(3, toks_ref, toks),
        local(4, slab_ref, slab),
        local(5, down_parts_ref.at[(place + 1) % line], down_own.at[0]),
        local(15, down_parts_ref.at[place], down_own.at[1]),
        local(16, grad_ref, dx_out),
        local(8, units_ref, units_sum),
        local(9, units_parts_ref.at[:, place], units_own_part),
    ]
    for copy in loads:
        copy.start()
    down_on = remote(DOWN_STEP, down_ref, down_in.at[0], (me, after))
    down_on.start()
    down_last = remote(DOWN_STEP + 1, down_own.at[0], down_in.at[1], (me, after))
    targets = [(side, mate), (side, beside), (side, corner)]
    targets += [(1 - side, head) for head in (me, mate, beside, corner)]
    homes = []
    for i, (to_side, to_head) in enumerate(targets):
        device = (to_head, at if i < 3 else other)
        source = units_sum.at[
            to_head, pl.ds(pl.multiple_of(to_side * w_rows, 16), w_rows)
        ]
        homes.append(remote(UNITS_HOME + i, source, units_in.at[side * 4 + me], device))
    units_own = local(
        10,
        units_sum.at[me, pl.ds(pl.multiple_of(side * w_rows, 16), w_rows)],
        units_in.at[side * 4 + me],
    )

    places = (side, place, line, (me, other), (me, after))

    def line_sum(which, part, got, hold, arrive):
        sems = [(line_sems.at[which, i, 0], line_sems.at[which, i, 1]) for i in (0, 1)]
        return LineSum(part, got, hold, arrive, sems, places, remote)

    query_line = line_sum(
        0, lambda b: query_part.at[:, b], query_got, query_hold, query_arrive
    )
    rest_line = line_sum(1, lambda b: rest_part.at[:, b], rest_got, rest_hold, rest_arrive)
    slab_line = line_sum(2, lambda b: slab.at[b], slab_got, slab_hold, slab_arrive)

    four_on = [remote(FOUR_ON + g, low.at[g, 0], four_in.at[g], (me, before)) for g in (0, 1)]
    two_on = [remote(TWO_ON + g, low.at[g, 1], two_in.at[g], (me, before)) for g in (0, 1)]

    def add_pair(g):
        def tile_of(step, carry):
            tile = pl.ds(pl.multiple_of(step * 128, 128), 128)
            got_three, got_one = three[g, tile, :].astype(F32), one[g, tile, :].astype(F32)
            to_four = jnp.where(side == 0, 0.0, got_three)
            to_two = jnp.where(side == 0, got_three, got_one)
            low[g, 0, tile, :] = (low[g, 0, tile, :].astype(F32) + to_four).astype(BF)
            low[g, 1, tile, :] = (low[g, 1, tile, :].astype(F32) + to_two).astype(BF)
            return carry

        lax.fori_loop(0, block // 128, tile_of, 0)
        four_on[g].start()

    def add_four(g):
        def tile_of(step, carry):
            tile = pl.ds(pl.multiple_of(step * 128, 128), 128)
            low[g, 1, tile, :] = (
                low[g, 1, tile, :].astype(F32) + four_in[g, tile, :].astype(F32)
            ).astype(BF)
            return carry

        four_on[g].wait_recv()
        lax.fori_loop(0, block // 128, tile_of, 0)
        two_on[g].start()

    for copy in low_loads + pair_loads:
        copy.wait()
    add_pair(0)

    head_gains[...] = jnp.zeros_like(head_gains)
    gain_rows[...] = jnp.zeros_like(gain_rows)
    loads[0].wait()
    loads[1].wait()

    def head_back(out, cols, tile, gain_tile, gain_row):
        value = raw[tile, cols]
        scale = head_scale(value)
        grad = out * cos_ref[tile, :] + swap_halves(out * sin_ref[tile, :])
        head_gains[0, gain_row : gain_row + 1, :] += jnp.sum(
            grad * value * scale, axis=0, keepdims=True
        )
        inner = grad * gain_tile
        mean = head_means(inner * value)
        return (scale * inner - value * (scale * scale * scale * mean)).astype(BF)

    def query_rows(step, carry):
        tile = pl.ds(pl.multiple_of(step * 64, 64), 64)
        for i in range(3):
            t = odd + i if i < 2 else 2 * (1 - odd)
            cols = pl.ds(pl.multiple_of(t * 128, 128), 128)
            if i < 2:
                out = dq_four_ref[tile, i * 128 : (i + 1) * 128]
            else:
                out = dq_two_ref[tile, :]
            grads[tile, cols] = head_back(out, cols, tile, query_gain_ref[...], 0)
        return carry

    lax.fori_loop(0, block // 64, query_rows, 0)
    three_on.wait_recv()
    one_on.wait_recv()
    add_pair(1)
    add_four(0)
    per_tile = 256 // w_rows
    tiles_per_head = count // per_tile

    def query_weights(step, carry):
        span = pl.ds(pl.multiple_of(step * 256, 256), 256)
        turned[span, :] = transposed(normed[:, span])
        first = pl.ds(step % tiles_per_head * per_tile, per_tile)
        part = nn(turned[span, :], grads[:, 0:COLS_Q])
        query_part[step // tiles_per_head, first] = part.astype(BF).reshape(
            per_tile, w_rows, COLS_Q
        )
        return carry

    lax.fori_loop(0, width // 256, query_weights, 0)
    query_line.start()
    add_four(1)
    loads[4].wait()
    slab_line.start()

    loads[3].wait()

    def token_scales(step, carry):
        tile = pl.ds(pl.multiple_of(step % (rows // 32) * 32, 32), 32)
        value = toks[step // (rows // 32), tile, :].astype(F32)
        scales[pl.ds(pl.multiple_of(step * 32, 32), 32), :] = lax.rsqrt(
            jnp.mean(value * value, axis=1, keepdims=True) + EPS
        )
        return carry

    lax.fori_loop(0, block // 32, token_scales, 0)
    loads[5].wait()
    down_on.wait_recv()

    def add_down(step, carry):
        span = pl.ds(pl.multiple_of(step * 256, 256), 256)
        down_own[0, :, span] = (
            down_own[0, :, span].astype(F32) + down_in[0, :, span].astype(F32)
        ).astype(BF)
        return carry

    lax.fori_loop(0, width // 256, add_down, 0)
    down_last.start()
    loads[8].wait()
    loads[9].wait()

    def add_units(step, carry):
        head, tile = step // (2 * w_rows // 16), step % (2 * w_rows // 16)
        tile = pl.ds(pl.multiple_of(tile * 16, 16), 16)
        total = units_sum[head, tile, :].astype(F32) + units_own_part[head, tile, :].astype(F32)
        units_sum[head, tile, :] = total.astype(BF)
        return carry

    lax.fori_loop(0, 8 * w_rows // 16, add_units, 0)
    query_line.step(1)
    for copy in two_on:
        copy.wait_recv()

    def key_rows(step, carry):
        tile = pl.ds(pl.multiple_of(step * 64, 64), 64)
        first_half = lanes((64, 128)) < HEAD
        both = []
        for g in (0, 1):
            from_pair = jnp.where(side == 0, one[g, tile, :].astype(F32), 0.0)
            both.append(own_refs[g][tile, :] + from_pair + two_in[g, tile, :].astype(F32))
        zero = jnp.where(odd == 0, both[0], both[1])
        unit = jnp.where(odd == 0, both[1], both[0])
        keys = jnp.where(first_half, zero, pltpu.roll(unit, HEAD, 1))
        values = jnp.where(first_half, pltpu.roll(zero, HEAD, 1), unit)
        cols = pl.ds(COLS_Q, 128)
        grads[tile, cols] = head_back(keys, cols, tile, key_gain_ref[...], 1)
        grads[tile, COLS_Q + 128 : COLS_Q + 256] = values.astype(BF)
        return carry

    lax.fori_loop(0, block // 64, key_rows, 0)

    loads[2].wait()

    def token_cols(step, carry):
        span = pl.ds(pl.multiple_of(step * 256, 256), 256)
        first = pl.ds(step % tiles_per_head * per_tile, per_tile)
        weight = w_in[step // tiles_per_head, first, :, 0:COLS_IN].reshape(256, COLS_IN)
        part = nt(grads[...], weight)
        parts[:, :, span] = part.astype(BF).reshape(4, rows, 256)
        value = toks[:, :, span].reshape(block, 256).astype(F32)
        gain_rows[0:1, span] = jnp.sum(part * value * scales[...], axis=0, keepdims=True)
        return carry

    lax.fori_loop(0, width // 256, token_cols, 0)
    to_mate = [
        remote(PART_CORNER, parts.at[corner], part_got.at[1], (mate, at)),
        remote(PART_MATE, parts.at[mate], part_got.at[0], (mate, at)),
    ]
    for copy in to_mate:
        copy.start()
    gain_rows[1:2, :] = gain_two_ref[...]

    def rest_weights(step, carry):
        span = pl.ds(pl.multiple_of(step * 256, 256), 256)
        first = pl.ds(step % tiles_per_head * per_tile, per_tile)
        head = step // tiles_per_head
        part = nn(turned[span, :], grads[:, COLS_Q : COLS_Q + 256])
        rest_part[head, first, :, 0:256] = part.astype(BF).reshape(per_tile, w_rows, 256)
        gain_cols = transposed(gain_rows[:, span])
        rest_part[head, first, :, 256:384] = gain_cols.astype(BF).reshape(per_tile, w_rows, 128)
        return carry

    lax.fori_loop(0, width // 256, rest_weights, 0)
    rest_line.start()
    for copy in homes:
        copy.start()
    units_own.start()
    slab_line.step(1)
    for step in range(2, line + 1):
        query_line.step(step, query_sum)
    query_home = [
        remote(QUERY_HOME + i, query_sum.at[to], query_in.at[me], (to, at))
        for i, to in enumerate((mate, beside, corner))
    ]
    query_own = local(13, query_sum.at[me], query_in.at[me])
    for copy in query_home:
        copy.start()
    query_own.start()
    to_mate[0].wait_recv()

    def add_part(step, carry):
        tile = pl.ds(pl.multiple_of(step * 32, 32), 32)
        parts[beside, tile, :] = (
            parts[beside, tile, :].astype(F32) + part_got[1, tile, :].astype(F32)
        ).astype(BF)
        return carry

    lax.fori_loop(0, rows // 32, add_part, 0)
    part_on = remote(PART_FAR, parts.at[beside], part_far, (beside, at))
    part_on.start()

    def gain_round(i):
        return remote(i, head_gains.at[i], gains_in.at[i], rounds[i], gain_sends, gain_recvs)

    rest_line.step(1)
    for i in range(len(rounds)):
        gain_round(i).start()
        gain_round(i).wait_recv()
        head_gains[i + 1] = head_gains[i] + gains_in[i]
        if i + 2 <= line:
            slab_line.step(i + 2, w_out_out)
            rest_line.step(i + 2, rest_sum)
    for step in range(len(rounds) + 2, line + 1):
        slab_line.step(step, w_out_out)
        rest_line.step(step, rest_sum)
    gains_out[...] = head_gains[len(rounds)]
    rest_home = [
        remote(REST_HOME + i, rest_sum.at[to], rest_in.at[me], (to, at))
        for i, to in enumerate((mate, beside, corner))
    ]
    rest_own = local(14, rest_sum.at[me], rest_in.at[me])
    for copy in rest_home:
        copy.start()
    rest_own.start()

    to_mate[1].wait_recv()
    part_on.wait_recv()
    loads[7].wait()

    def norm_back(step, carry):
        tile = pl.ds(pl.multiple_of(step * 32, 32), 32)
        grad = (
            parts[me, tile, :].astype(F32)
            + part_got[0, tile, :].astype(F32)
            + part_far[tile, :].astype(F32)
        )
        value = toks[me, tile, :].astype(F32)
        scale = lax.rsqrt(jnp.mean(value * value, axis=1, keepdims=True) + EPS)
        inner = grad * gain_ref[0:1, :]
        mean = jnp.mean(inner * value, axis=1, keepdims=True)
        dx_out[tile, :] += scale * inner - value * (scale * scale * scale * mean)
        return carry

    lax.fori_loop(0, rows // 32, norm_back, 0)

    loads[6].wait()
    down_last.wait_recv()

    def down_rows(step, carry):
        span = pl.ds(pl.multiple_of(step * 256, 256), 256)
        down_out[:, span] = down_own[1, :, span].astype(F32) + down_in[1, :, span].astype(F32)
        return carry

    lax.fori_loop(0, width // 256, down_rows, 0)
    for copy in homes:
        copy.wait()
    units_own.wait()
    units = units_ref.shape[2] // 2
    ff_rows = units // line
    for j, out in enumerate((gate_out, up_out)):
        for head in range(4):
            sides = [
                units_in[4 * of_side + head, :, j * units : (j + 1) * units].astype(F32)
                for of_side in range(2)
            ]
            pieces = [
                sides[p % 2][:, p // 2 * ff_rows : (p // 2 + 1) * ff_rows]
                for p in range(2 * line)
            ]
            out[:, 2 * units * head : 2 * units * (head + 1)] = jnp.concatenate(pieces, axis=1)
    for copy in query_home:
        copy.wait()
    query_own.wait()
    for g in range(4):
        query_out[:, g * COLS_Q : (g + 1) * COLS_Q] = query_in[g].astype(F32)
    for copy in rest_home:
        copy.wait()
    rest_own.wait()
    first_half = lanes((w_rows, 128)) < HEAD
    for j, out in enumerate((key_out, value_out)):
        tiles = [rest_in[g, :, j * 128 : (j + 1) * 128].astype(F32) for g in range(4)]
        moved = [pltpu.roll(tile, HEAD, 1) for tile in tiles]
        out[:, 0:128] = tiles[0] + jnp.where(first_half, 0.0, moved[1])
        out[:, 128:256] = jnp.where(first_half, moved[1], moved[2])
        out[:, 256:384] = tiles[3] + jnp.where(first_half, moved[2], 0.0)
    norm_out[...] = (
        rest_in[0, :, 256:384].astype(F32)
        + rest_in[1, :, 256:384].astype(F32)
        + rest_in[2, :, 256:384].astype(F32)
        + rest_in[3, :, 256:384].astype(F32)
    )
    for copy in four_on + two_on + to_mate:
        copy.wait_send()
    for copy in (three_on, one_on, down_on, down_last, part_on):
        copy.wait_send()
    for total in (query_line, rest_line, slab_line):
        total.drain()
    for i in range(len(rounds)):
        gain_round(i).wait_send()


def last(
    dq, dkv_low, dkv_own, pair_four, raw, cosine, sine, query_gain, key_gain, normed, w_in, toks,
    gains, gain_two, units, units_parts, down, down_parts, slab, grad,
):
    _, rows, width = toks.shape
    _, count, w_rows, _ = w_in.shape
    line = count // 2
    block = 4 * rows
    anywhere = pl.BlockSpec(memory_space=pl.ANY)
    vmem = pl.BlockSpec(memory_space=pltpu.VMEM)
    shape = jax.ShapeDtypeStruct
    dma = pltpu.SemaphoreType.DMA
    rounds = 3 + int(math.log2(line))
    part = (4, w_rows, COLS_Q)
    out_rows = slab.shape[1]
    return pl.pallas_call(
        functools.partial(last_kernel, line),
        out_shape=(
            shape((rows, width), F32),
            shape((w_rows, 4 * COLS_Q), F32),
            shape((w_rows, KVHEADS * HEAD), F32),
            shape((w_rows, KVHEADS * HEAD), F32),
            shape((w_rows, 128), F32),
            shape((w_rows, 4 * units.shape[2]), F32),
            shape((w_rows, 4 * units.shape[2]), F32),
            shape(down.shape, F32),
            shape((out_rows, width), F32),
            shape((8, 128), F32),
        ),
        in_specs=[vmem] * 2 + [anywhere] * 2 + [vmem] * 2 + [anywhere] * 2 + [vmem] * 4
        + [anywhere] * 3 + [vmem] * 2 + [anywhere] * 6,
        out_specs=(vmem,) * 10,
        scratch_shapes=[
            pltpu.VMEM((2, 2, block, 128), BF),
            pltpu.VMEM((2, block, 128), BF),
            pltpu.VMEM((2, block, 128), BF),
            pltpu.VMEM((2, block, 128), BF),
            pltpu.VMEM((2, block, 128), BF),
            pltpu.VMEM((block, COLS_Q + 128), F32),
            pltpu.VMEM((block, width), BF),
            pltpu.VMEM((width, block), BF),
            pltpu.VMEM(w_in.shape, BF),
            pltpu.VMEM(toks.shape, BF),
            pltpu.VMEM((block, 1), F32),
            pltpu.VMEM((block, COLS_IN), BF),
            pltpu.VMEM((4, count, w_rows, COLS_Q), BF),
            pltpu.VMEM((4, count, w_rows, COLS_Q), BF),
            pltpu.VMEM((line,) + part, BF),
            pltpu.VMEM((line,) + part, BF),
            pltpu.VMEM((line - 1,) + part, BF),
            pltpu.VMEM((line - 1,) + part, BF),
            pltpu.VMEM((line - 1,) + part, BF),
            pltpu.VMEM((line - 1,) + part, BF),
            pltpu.VMEM(part, BF),
            pltpu.VMEM(part, BF),
            pltpu.VMEM(slab.shape, BF),
            pltpu.VMEM((line,) + slab.shape[1:], BF),
            pltpu.VMEM((line - 1,) + slab.shape[1:], BF),
            pltpu.VMEM((line - 1,) + slab.shape[1:], BF),
            pltpu.VMEM(units.shape, BF),
            pltpu.VMEM((8, w_rows, units.shape[2]), BF),
            pltpu.VMEM(part, BF),
            pltpu.VMEM(part, BF),
            pltpu.VMEM((2,) + down.shape, BF),
            pltpu.VMEM((2,) + down.shape, BF),
            pltpu.VMEM((4, rows, width), BF),
            pltpu.VMEM((2, rows, width), BF),
            pltpu.VMEM((rows, width), BF),
            pltpu.VMEM((128, width), F32),
            pltpu.VMEM((rounds + 1, 8, 128), F32),
            pltpu.VMEM((rounds, 8, 128), F32),
            dma((LAST_TRANSFERS,)),
            dma((LAST_TRANSFERS,)),
            dma((3, 2, 2, line)),
            dma((rounds,)),
            dma((rounds,)),
            dma((17,)),
        ],
        compiler_params=pltpu.CompilerParams(
            collective_id=3, has_side_effects=True, vmem_limit_bytes=58 << 20
        ),
        cost_estimate=pl.CostEstimate(
            flops=60_000_000_000, bytes_accessed=60_000_000, transcendentals=1_000_000
        ),
        name="last",
    )(
        *dq, *dkv_low, *dkv_own, pair_four, raw, cosine, sine, query_gain, key_gain, normed, w_in,
        toks, gains, gain_two, units, units_parts, down, down_parts, slab, grad,
    )


def shards(
    tokens,
    doc_lengths,
    norm1_gain,
    w_query,
    w_key,
    w_value,
    query_gain,
    key_gain,
    w_out,
    norm2_gain,
    w_gate,
    w_up,
    w_down,
    cotangent,
):
    tok_rows, width = tokens.shape
    blocks = lax.axis_size("blk")
    groups = lax.axis_size("head")
    group_id = lax.axis_index("head")
    blk_place = lax.axis_index("blk")
    block_len = groups * tok_rows
    per_group = QHEADS // groups
    head_ratio = QHEADS // KVHEADS
    w_rows = w_query.shape[0]
    line = blocks // 2
    side = blk_place % 2
    ff_rows = w_down.shape[0]
    ff_cols = line * ff_rows
    q_cols = per_group * HEAD
    firsts = [g * per_group // head_ratio for g in range(groups)]
    odd = group_id % 2

    starts = jnp.cumsum(doc_lengths) - doc_lengths
    offsets = jnp.arange(block_len, dtype=jnp.int32)
    token_pos = blk_place * block_len + offsets
    inside = starts[None, :] <= token_pos[:, None]
    token_start = jnp.max(jnp.where(inside, starts[None, :], 0), axis=1)
    in_doc = token_pos - token_start
    rope_freq = jnp.exp(-math.log(10000.0) * jnp.arange(HEAD // 2, dtype=F32) / (HEAD // 2))
    rope_angle = in_doc.astype(F32)[:, None] * rope_freq[None, :]
    cosine, sine = jnp.cos(rope_angle), jnp.sin(rope_angle)
    cosine = jnp.concatenate([cosine] * 4, axis=1)
    sine = jnp.concatenate([-sine, sine] * 2, axis=1)
    window_start = token_start - (blk_place - BACK) * block_len
    tiles = block_len // TILE
    edges = jnp.stack(
        [window_start[::TILE], window_start[TILE - 1 :: TILE]], axis=1
    ).reshape(2 * tiles)
    meta = jnp.concatenate([odd[None].astype(jnp.int32), edges.astype(jnp.int32)])

    rest = []
    for g in range(groups):
        kv = slice(firsts[g] * HEAD, (firsts[g] + 2) * HEAD)
        rest += [
            w_key[:, kv],
            w_value[:, kv],
            norm1_gain[:, None],
            norm2_gain[:, None],
            jnp.zeros((w_rows, 126), BF),
        ]
    rest = jnp.concatenate(rest, axis=1).reshape(w_rows, groups, COLS_Q)
    rest = jnp.swapaxes(rest, 0, 1)
    query_row = jnp.concatenate([query_gain, query_gain]).astype(F32)[None, :]
    key_row = jnp.concatenate([key_gain, key_gain]).astype(F32)[None, :]
    (
        wide,
        queries,
        kv_window,
        raw,
        normed_one,
        w_in,
        top_far,
        w_blk,
        slab,
        slab_next,
        down_next,
        toks,
        gains,
    ) = first(
        tokens,
        w_query,
        rest,
        w_gate,
        w_up,
        w_down,
        w_out,
        cotangent,
        cosine,
        sine,
        query_row,
        key_row,
    )
    slabs, downs = [slab, slab_next], [w_down, down_next]
    for _ in range(line - 4):
        slabs.append(ring(slabs[-1], 2))
        downs.append(ring(downs[-1], 2))
    w_own = w_blk.reshape(q_cols, width)
    slabs, downs, w_own, top_far, top_own, queries = sync(
        slabs, downs, w_own, top_far, cotangent, queries
    )
    slabs.append(ring(slabs[-1], 2))
    downs.append(ring(downs[-1], 2))
    w_far = swap(w_own, "head", 2)
    top_across = swap(top_own, "blk", 1)
    top_corner = swap(top_far, "blk", 1)
    kept, attn_out = attend(meta, wide, kv_window, window_start[:, None])
    kept, attn_out, slabs, downs, w_far, top_across, top_corner = sync(
        kept, attn_out, slabs, downs, w_far, top_across, top_corner
    )
    if ff_rows % 16:
        downs.append(ring(downs[-1], 2))
        w_d = jnp.zeros((line, ff_rows, width), BF)
        for step, part in enumerate(downs):
            w_d = put(w_d, part, (blk_place // 2 - step) % line)
        downs = [w_d.reshape(ff_cols, width)]
    attn_out = attn_out.reshape(groups, tok_rows, q_cols)

    (
        resid,
        grad_resid,
        grad_attn,
        mixed,
        grad_mix,
        _,
        _,
        _,
        gu_parts,
        gu_moved,
        down_parts,
        weight_own,
        weight_in,
        out_own,
        out_far,
        out_across,
        out_corner,
        grad_gain_two,
    ) = middle(
        attn_out,
        tokens,
        w_own,
        w_far,
        gains[1:2],
        (cotangent, top_far, top_across, top_corner),
        slabs,
        downs,
    )
    down_parts = down_parts.reshape(line, ff_rows, width)
    gu_parts = gu_parts.reshape(groups, line, 2 * w_rows, 2 * ff_cols)
    down_sum = LineScatter(lambda p: take(down_parts, p))
    gu_sum = LineScatter(lambda p: take(gu_parts, p, 1))
    gu_sum.total = gu_moved
    gu_sum.add()
    down_sum.ahead(line - 4)
    gu_sum.ahead(line - 4)
    down_moved, gu_moved = down_sum.send(), gu_sum.send()

    out_far = swap(out_far, "head", 2)
    out_across = swap(out_across, "blk", 1)
    out_corner = lax.ppermute(
        out_corner,
        ("head", "blk"),
        [(i, (i // blocks ^ 2) * blocks + (i % blocks ^ 1)) for i in range(groups * blocks)],
    )
    back = functools.partial(
        attend_back,
        meta=meta,
        wide=wide,
        queries=queries,
        kv=kv_window,
        kept=kept,
        grads=grad_mix.reshape(block_len, q_cols),
        starts=window_start[None, :],
    )
    four = back(0)
    four, down_moved, gu_moved, out_far, out_across, out_corner, kv_window = sync(
        four, down_moved, gu_moved, out_far, out_across, out_corner, kv_window
    )
    down_sum.total, gu_sum.total = down_moved, gu_moved
    down_sum.add()
    gu_sum.add()
    gu_moved = gu_sum.send()
    pair_four = swap(four[1][2:], "blk", 1)
    slab_far = swap((weight_own[1].astype(F32) + weight_in[1].astype(F32)).astype(BF), "head", 2)
    two = back(1, kv=kv_window)
    four, two, gu_moved, pair_four, slab_far = sync(four, two, gu_moved, pair_four, slab_far)
    out_act = (
        resid
        + out_own.astype(F32)
        + out_far.astype(F32)
        + out_across.astype(F32)
        + out_corner.astype(F32)
    ).astype(BF)
    out_slab = weight_own[0].astype(F32) + weight_in[0].astype(F32) + slab_far.astype(F32)
    out_slab = out_slab.astype(BF).reshape(blocks, w_out.shape[0], width)
    (
        d_tokens,
        d_w_query,
        d_w_key,
        d_w_value,
        norm_gains,
        d_w_gate,
        d_w_up,
        d_w_down,
        d_w_out,
        head_gains,
    ) = last(
        (four[0], two[0]),
        (four[1], two[1]),
        (four[2], two[2]),
        pair_four,
        raw,
        cosine,
        sine,
        query_row,
        key_row,
        normed_one,
        w_in,
        toks,
        gains,
        grad_gain_two,
        gu_moved,
        gu_parts,
        down_sum.total.astype(BF),
        down_parts,
        out_slab,
        grad_resid,
    )
    gain_sums = head_gains[:2, :HEAD] + head_gains[:2, HEAD:]
    d_norm1_gain, d_norm2_gain = norm_gains[:, 0], norm_gains[:, 1]
    return (
        out_act,
        d_tokens,
        d_norm1_gain,
        d_w_query,
        d_w_key,
        d_w_value,
        gain_sums[0],
        gain_sums[1],
        d_w_out,
        d_norm2_gain,
        d_w_gate,
        d_w_up,
        d_w_down,
    )


def solution(mesh):
    by_token = P(("blk", "head"), None)
    by_row = P(("head", "blk"), None)
    by_entry = P(("head", "blk"))
    in_specs = (
        by_token,
        P(),
        by_entry,
        by_row,
        by_row,
        by_row,
        P(),
        P(),
        by_row,
        by_entry,
        by_row,
        by_row,
        by_row,
        by_token,
    )
    out_specs = (
        by_token,
        by_token,
        by_entry,
        by_row,
        by_row,
        by_row,
        P(),
        P(),
        by_row,
        by_entry,
        by_row,
        by_row,
        by_row,
    )
    return jax.shard_map(shards, mesh=mesh, in_specs=in_specs, out_specs=out_specs, check_vma=False)
```

profile of v0, /device:TPU:17, one launch (start us, length us, event | category | flops | bytes accessed | tf_op | source)
XLA Modules:
  0.0 588.9 jit_solution(14304588045532937873)
XLA Ops:
  3.7 0.9 fusion.6
  5.0 1.9 fusion.5
  7.0 0.9 pad_maximum_fusion
  8.0 119.9 %first.1 = (bf16[6,1024,128]{2,1,0:T(8,128)(2,1)}, bf16[6,1024,128]{2,1,0:T(8,128)(2,1)}, bf16[5,2,1024,128]{3,2,1,0:T(8,128)(2,1)}, f32[1024,512]{1,0:T(8,128)}...) custom-call(bf16[256,2048]{1,0:T(8,128)(2,1)} %tokens_ref.3, ...), custom_call_target="tpu_custom_call" | custom-call | flops 60000002048 | bytes 60000000 | tf_op jit(solution)/shard_map/first/pallas_call | solution.py:1394
  128.1 1.4 collective-permute-start.1
  129.5 1.1 collective-permute-start.2
  130.5 1.5 collective-permute-start.4
  132.7 1.7 copy-done.15
  134.4 1.4 copy-done.16
  135.8 37.3 %attend.1 = (f32[6,1024,128]{2,1,0:T(8,128)}, bf16[1024,384]{1,0:T(8,128)(2,1)S(1)}) custom-call(s32[9]{0:T(128)S(1)} %pad_add_fusion.1.meta_ref, bf16[6,1024,128]{2,1,0:T(8,128)(2,1)S(1)} %copy-done.16, bf16[5,2,1024,128]{3,2,1,0:T(8,128)(2,1)S(1)} %copy-done.15, s32[1024,1]{1,0:T(8,128)S(1)} %copy.72.start_ref), custom_call_target="tpu_custom_call" | custom-call | flops 60000002048 | bytes 20000000 | tf_op jit(solution)/shard_map/attend/pallas_call | solution.py:226
  173.2 0.9 copy-done.13
  174.7 154.1 %middle.1 = (f32[256,2048]{1,0:T(8,128)}, f32[256,2048]{1,0:T(8,128)}, bf16[256,2048]{1,0:T(8,128)(2,1)}, bf16[256,1536]{1,0:T(8,128)(2,1)}, bf16[4,256,384]{2,1...) custom-call(bf16[4,256,384]{2,1,0:T(8,128)(2,1)} %bitcast.52, ...), custom_call_target="tpu_custom_call" | custom-call | flops 60000002048 | bytes 100000000 | tf_op jit(solution)/shard_map/middle/pallas_call | solution.py:971
  328.8 2.1 dynamic-slice_bitcast_fusion
  330.9 5.3 collective-permute-start.5
  336.2 1.6 fusion.2
  339.6 1.1 collective-permute-start.9
  340.8 51.9 %attend_back_four.1 = (f32[1024,256]{1,0:T(8,128)S(1)}, bf16[4,1024,128]{2,1,0:T(8,128)(2,1)S(1)}, f32[1024,128]{1,0:T(8,128)S(1)}) custom-call(s32[9]{0:T(128)S(1)} %pad_add_fusion.1.meta_ref, bf16[6,1024,128]{2,1,0:T(8,128)(2,1)S(1)} %copy-done.17, bf16[6,1024,128]{2,1,0:T(8,128)(2,1)} %get-tuple-element.124.query_ref, ...), custom_call_target="tpu_custom_call" | custom-call | flops 80000000000 | bytes 40000000 | tf_op jit(solution)/shard_map/attend_back_four/pallas_call | solution.py:384
  392.7 2.0 fusion.3
  394.6 0.9 collective-permute-start.12
  395.5 2.7 fusion.1
  398.2 30.8 %attend_back_two.1 = (f32[1024,128]{1,0:T(8,128)S(1)}, bf16[4,1024,128]{2,1,0:T(8,128)(2,1)S(1)}, f32[1024,128]{1,0:T(8,128)S(1)}) custom-call(s32[9]{0:T(128)S(1)} %pad_add_fusion.1.meta_ref, bf16[6,1024,128]{2,1,0:T(8,128)(2,1)S(1)} %copy-done.17, bf16[6,1024,128]{2,1,0:T(8,128)(2,1)S(1)} %copy-done.18, ...), custom_call_target="tpu_custom_call" | custom-call | flops 40000000000 | bytes 40000000 | tf_op jit(solution)/shard_map/attend_back_two/pallas_call | solution.py:384
  429.1 8.1 %collective-permute-start.11 = (bf16[2,1024,128]{2,1,0:T(8,128)(2,1)S(1)}, bf16[2,1024,128]{2,1,0:T(8,128)(2,1)S(1)}, u32[]{:S(2)}, u32[]{:S(2)}) collective-permute-start(bf16[2,1024,128]{2,1,0:T(8,128)(2,1)S(1)} %slice.77), channel_id=1, source_target_pairs={{0,1},{1,0},{2,3},{3,2},{4,5},{5,4},{6,7},{7,6},{8,9},{9,8},{10,11... | collective-permute-start | bytes 1572872 | tf_op jit(solution)/shard_map/ppermute | solution.py:44
  437.3 4.0 add_convert_fusion.1
  441.3 2.1 fusion.4.down_ref
  443.4 3.4 collective-permute-done.11.pair_four_ref
  446.9 3.7 fusion
  450.6 125.8 %last.1 = (f32[256,2048]{1,0:T(8,128)}, f32[64,1536]{1,0:T(8,128)}, f32[64,384]{1,0:T(8,128)}, f32[64,384]{1,0:T(8,128)}, f32[64,128]{1,0:T(8,128)}, /*index=5*/...) custom-call(f32[1024,256]{1,0:T(8,128)} %copy-done.20, ...), custom_call_target="tpu_custom_call" | custom-call | flops 60000002048 | bytes 60000000 | tf_op jit(solution)/shard_map/last/pallas_call | solution.py:2000
  576.4 1.5 slice_reduce_fusion
  579.3 3.3 copy.86
  585.3 1.1 copy.91
  586.4 1.1 copy.92
  587.5 1.1 copy.93
  (120 shorter events, 10.9 us)
Async XLA Ops:
  0.6 6.3 %copy-start.35 = (bf16[64]{0:T(256)(128)(2,1)S(1)}, bf16[64]{0:T(256)(128)(2,1)}, u32[]{:S(2)}) copy-start(bf16[64]{0:T(256)(128)(2,1)} %param.20) | copy-start | bytes 388
  7.0 120.9 %copy-start.4 = (f32[1,128]{1,0:T(1,128)}, f32[1,128]{1,0:T(1,128)S(1)}, u32[]{:S(2)}) copy-start(f32[1,128]{1,0:T(1,128)S(1)} %get-tuple-element.198.query_gain_ref) | copy-start | bytes 1540
  7.0 120.9 %copy-start.5 = (f32[1,128]{1,0:T(1,128)}, f32[1,128]{1,0:T(1,128)S(1)}, u32[]{:S(2)}) copy-start(f32[1,128]{1,0:T(1,128)S(1)} %get-tuple-element.199.key_gain_ref) | copy-start | bytes 1540
  7.9 120.1 %copy-start = (f32[1024,128]{1,0:T(8,128)}, f32[1024,128]{1,0:T(8,128)S(1)}, u32[]{:S(2)}) copy-start(f32[1024,128]{1,0:T(8,128)S(1)} %get-tuple-element.196.cos_ref) | copy-start | bytes 1572868
  7.9 120.1 %copy-start.1 = (f32[1024,128]{1,0:T(8,128)}, f32[1024,128]{1,0:T(8,128)S(1)}, u32[]{:S(2)}) copy-start(f32[1024,128]{1,0:T(8,128)S(1)} %get-tuple-element.197.sin_ref) | copy-start | bytes 1572868
  8.0 122.6 %copy-start.37 = (bf16[256,2048]{1,0:T(8,128)(2,1)S(1)}, bf16[256,2048]{1,0:T(8,128)(2,1)}, u32[]{:S(2)}) copy-start(bf16[256,2048]{1,0:T(8,128)(2,1)} %top_ref.3) | copy-start | bytes 3145732
  128.0 45.2 %copy-start.6 = (bf16[256,2048]{1,0:T(8,128)(2,1)}, bf16[256,2048]{1,0:T(8,128)(2,1)S(1)}, u32[]{:S(2)}) copy-start(bf16[256,2048]{1,0:T(8,128)(2,1)S(1)} %get-tuple-element.110.top_far_ref) | copy-start | bytes 3145732
  128.0 45.2 %copy-start.10 = (bf16[160,2048]{1,0:T(8,128)(2,1)}, bf16[160,2048]{1,0:T(8,128)(2,1)S(1)}, u32[]{:S(2)}) copy-start(bf16[160,2048]{1,0:T(8,128)(2,1)S(1)} %get-tuple-element.120.refs_4_) | copy-start | bytes 1966084
  128.0 46.1 %copy-start.3 = (f32[8,2048]{1,0:T(8,128)}, f32[8,2048]{1,0:T(8,128)S(1)}, u32[]{:S(2)}) copy-start(f32[8,2048]{1,0:T(8,128)S(1)} %get-tuple-element.113.gain_ref) | copy-start | bytes 196612
  128.0 46.7 %collective-permute-start = (bf16[4,128,1280]{2,1,0:T(8,128)(2,1)}, bf16[4,128,1280]{2,1,0:T(8,128)(2,1)}, u32[]{:S(2)}, u32[]{:S(2)}) collective-permute-start(bf16[4,128,1280]{2,1,0:T(8,128)(2,1)} %get-tuple-element.117.refs_1_), channel_id=1, source_target_pairs={{0,2},{1,3},{2,4},{3,5},{4,6},{5,7},{6,0},{7,1},{8,10},{9,11},{10,... | collective-permute-start | bytes 3932168 | tf_op jit(solution)/shard_map/ppermute | solution.py:49
  128.1 46.6 %collective-permute-start.1 = (bf16[160,2048]{1,0:T(8,128)(2,1)S(1)}, bf16[160,2048]{1,0:T(8,128)(2,1)}, u32[]{:S(2)}, u32[]{:S(2)}) collective-permute-start(bf16[160,2048]{1,0:T(8,128)(2,1)S(1)} %get-tuple-element.120.refs_4_), channel_id=1, source_target_pairs={{0,2},{1,3},{2,4},{3,5},{4,6},{5,7},{6,0},{7,1},{8,10},{9,11},{10,... | collective-permute-start | bytes 1966088 | tf_op jit(solution)/shard_map/ppermute | solution.py:49
  129.5 45.2 %collective-permute-start.2 = (bf16[384,2048]{1,0:T(8,128)(2,1)}, bf16[384,2048]{1,0:T(8,128)(2,1)}, u32[]{:S(2)}, u32[]{:S(2)}) collective-permute-start(bf16[384,2048]{1,0:T(8,128)(2,1)} %bitcast.69), channel_id=1, source_target_pairs={{0,16},{8,24},{16,0},{24,8},{1,17},{9,25},{17,1},{25,9},{2,18},{10... | collective-permute-start | bytes 4718600 | tf_op jit(solution)/shard_map/ppermute | solution.py:44
  130.5 44.1 %collective-permute-start.3 = (bf16[256,2048]{1,0:T(8,128)(2,1)S(1)}, bf16[256,2048]{1,0:T(8,128)(2,1)}, u32[]{:S(2)}, u32[]{:S(2)}) collective-permute-start(bf16[256,2048]{1,0:T(8,128)(2,1)S(1)} %copy-done.37), channel_id=1, source_target_pairs={{0,1},{1,0},{2,3},{3,2},{4,5},{5,4},{6,7},{7,6},{8,9},{9,8},{10,11... | collective-permute-start | bytes 3145736 | tf_op jit(solution)/shard_map/ppermute | solution.py:44
  130.5 44.1 %collective-permute-start.4 = (bf16[256,2048]{1,0:T(8,128)(2,1)S(1)}, bf16[256,2048]{1,0:T(8,128)(2,1)}, u32[]{:S(2)}, u32[]{:S(2)}) collective-permute-start(bf16[256,2048]{1,0:T(8,128)(2,1)S(1)} %get-tuple-element.110.top_far_ref), channel_id=1, source_target_pairs={{0,1},{1,0},{2,3},{3,2},{4,5},{5,4},{6,7},{7,6},{8,9},{9,8},{10,11... | collective-permute-start | bytes 3145736 | tf_op jit(solution)/shard_map/ppermute | solution.py:44
  328.8 7.4 %copy-start.30 = (bf16[4,128,1280]{2,1,0:T(8,128)(2,1)S(1)}, bf16[4,128,1280]{2,1,0:T(8,128)(2,1)}, u32[]{:S(2)}) copy-start(bf16[4,128,1280]{2,1,0:T(8,128)(2,1)} %get-tuple-element.131) | copy-start | bytes 3932164
  330.9 9.8 %copy-start.14 = (bf16[4,256,384]{2,1,0:T(8,128)(2,1)S(1)}, bf16[4,256,384]{2,1,0:T(8,128)(2,1)}, u32[]{:S(2)}) copy-start(bf16[4,256,384]{2,1,0:T(8,128)(2,1)} %get-tuple-element.126) | copy-start | bytes 2359300
  330.9 9.8 %copy-start.17 = (bf16[6,1024,128]{2,1,0:T(8,128)(2,1)S(1)}, bf16[6,1024,128]{2,1,0:T(8,128)(2,1)}, u32[]{:S(2)}) copy-start(bf16[6,1024,128]{2,1,0:T(8,128)(2,1)} %get-tuple-element.94.query_ref.wide_ref) | copy-start | bytes 4718596
  330.9 63.7 %collective-permute-start.5 = (bf16[160,2048]{1,0:T(8,128)(2,1)}, bf16[160,2048]{1,0:T(8,128)(2,1)S(1)}, u32[]{:S(2)}, u32[]{:S(2)}) collective-permute-start(bf16[160,2048]{1,0:T(8,128)(2,1)} %dynamic-slice_bitcast_fusion), channel_id=1, source_target_pairs={{0,2},{1,3},{2,4},{3,5},{4,6},{5,7},{6,0},{7,1},{8,10},{9,11},{10,... | collective-permute-start | bytes 1966088 | tf_op jit(solution)/shard_map/ppermute | solution.py:49
  337.8 57.7 %collective-permute-start.6 = (bf16[4,128,1280]{2,1,0:T(8,128)(2,1)S(1)}, bf16[4,128,1280]{2,1,0:T(8,128)(2,1)S(1)}, u32[]{:S(2)}, u32[]{:S(2)}) collective-permute-start(bf16[4,128,1280]{2,1,0:T(8,128)(2,1)S(1)} %fusion.2), channel_id=1, source_target_pairs={{0,2},{1,3},{2,4},{3,5},{4,6},{5,7},{6,0},{7,1},{8,10},{9,11},{10,... | collective-permute-start | bytes 3932168 | tf_op jit(solution)/shard_map/ppermute | solution.py:49
  338.1 57.4 %collective-permute-start.7 = (bf16[256,2048]{1,0:T(8,128)(2,1)}, bf16[256,2048]{1,0:T(8,128)(2,1)}, u32[]{:S(2)}, u32[]{:S(2)}) collective-permute-start(bf16[256,2048]{1,0:T(8,128)(2,1)} %get-tuple-element.133), channel_id=1, source_target_pairs={{0,16},{8,24},{16,0},{24,8},{1,17},{9,25},{17,1},{25,9},{2,18},{10... | collective-permute-start | bytes 3145736 | tf_op jit(solution)/shard_map/ppermute | solution.py:44
  338.9 56.6 %collective-permute-start.8 = (bf16[256,2048]{1,0:T(8,128)(2,1)}, bf16[256,2048]{1,0:T(8,128)(2,1)}, u32[]{:S(2)}, u32[]{:S(2)}) collective-permute-start(bf16[256,2048]{1,0:T(8,128)(2,1)} %get-tuple-element.134), channel_id=1, source_target_pairs={{0,1},{1,0},{2,3},{3,2},{4,5},{5,4},{6,7},{7,6},{8,9},{9,8},{10,11... | collective-permute-start | bytes 3145736 | tf_op jit(solution)/shard_map/ppermute | solution.py:44
  339.6 55.9 %collective-permute-start.9 = (bf16[256,2048]{1,0:T(8,128)(2,1)}, bf16[256,2048]{1,0:T(8,128)(2,1)}, u32[]{:S(2)}, u32[]{:S(2)}) collective-permute-start(bf16[256,2048]{1,0:T(8,128)(2,1)} %get-tuple-element.135), channel_id=1, source_target_pairs={{0,17},{1,16},{2,19},{3,18},{4,21},{5,20},{6,23},{7,22},{8,25},{9,... | collective-permute-start | bytes 3145736 | tf_op jit(solution)/shard_map/ppermute | solution.py:2235
  340.8 51.9 %copy-start.24 = (bf16[2,384,2048]{2,1,0:T(8,128)(2,1)S(1)}, bf16[2,384,2048]{2,1,0:T(8,128)(2,1)}, u32[]{:S(2)}) copy-start(bf16[2,384,2048]{2,1,0:T(8,128)(2,1)} %get-tuple-element.147) | copy-start | bytes 9437188
  340.8 51.9 %copy-start.25 = (bf16[2,384,2048]{2,1,0:T(8,128)(2,1)S(1)}, bf16[2,384,2048]{2,1,0:T(8,128)(2,1)}, u32[]{:S(2)}) copy-start(bf16[2,384,2048]{2,1,0:T(8,128)(2,1)} %get-tuple-element.148) | copy-start | bytes 9437188
  392.6 36.4 %copy-start.2 = (bf16[4,1024,128]{2,1,0:T(8,128)(2,1)}, bf16[4,1024,128]{2,1,0:T(8,128)(2,1)S(1)}, u32[]{:S(2)}) copy-start(bf16[4,1024,128]{2,1,0:T(8,128)(2,1)S(1)} %get-tuple-element.151.low_four_ref) | copy-start | bytes 3145732
  394.6 48.8 %collective-permute-start.12 = (bf16[384,2048]{1,0:T(8,128)(2,1)}, bf16[384,2048]{1,0:T(8,128)(2,1)}, u32[]{:S(2)}, u32[]{:S(2)}) collective-permute-start(bf16[384,2048]{1,0:T(8,128)(2,1)} %fusion.3), channel_id=1, source_target_pairs={{0,16},{8,24},{16,0},{24,8},{1,17},{9,25},{17,1},{25,9},{2,18},{10... | collective-permute-start | bytes 4718600 | tf_op jit(solution)/shard_map/ppermute | solution.py:44
  398.2 48.7 %collective-permute-start.10 = (bf16[4,128,1280]{2,1,0:T(8,128)(2,1)}, bf16[4,128,1280]{2,1,0:T(8,128)(2,1)}, u32[]{:S(2)}, u32[]{:S(2)}) collective-permute-start(bf16[4,128,1280]{2,1,0:T(8,128)(2,1)} %fusion.1), channel_id=1, source_target_pairs={{0,2},{1,3},{2,4},{3,5},{4,6},{5,7},{6,0},{7,1},{8,10},{9,11},{10,... | collective-permute-start | bytes 3932168 | tf_op jit(solution)/shard_map/ppermute | solution.py:49
  398.2 39.0 %copy-start.26 = (f32[256,2048]{1,0:T(8,128)S(1)}, f32[256,2048]{1,0:T(8,128)}, u32[]{:S(2)}) copy-start(f32[256,2048]{1,0:T(8,128)} %get-tuple-element.122) | copy-start | bytes 6291460
  429.1 12.3 %copy-start.19 = (bf16[4,1024,128]{2,1,0:T(8,128)(2,1)}, bf16[4,1024,128]{2,1,0:T(8,128)(2,1)S(1)}, u32[]{:S(2)}) copy-start(bf16[4,1024,128]{2,1,0:T(8,128)(2,1)S(1)} %get-tuple-element.152.low_two_ref) | copy-start | bytes 3145732
  429.1 12.3 %copy-start.21 = (f32[1024,128]{1,0:T(8,128)}, f32[1024,128]{1,0:T(8,128)S(1)}, u32[]{:S(2)}) copy-start(f32[1024,128]{1,0:T(8,128)S(1)} %get-tuple-element.150.dq_two_ref) | copy-start | bytes 1572868
  429.1 12.2 %copy-start.22 = (f32[1024,128]{1,0:T(8,128)}, f32[1024,128]{1,0:T(8,128)S(1)}, u32[]{:S(2)}) copy-start(f32[1024,128]{1,0:T(8,128)S(1)} %get-tuple-element.154.own_two_ref) | copy-start | bytes 1572868
  429.1 17.7 %collective-permute-start.11 = (bf16[2,1024,128]{2,1,0:T(8,128)(2,1)S(1)}, bf16[2,1024,128]{2,1,0:T(8,128)(2,1)S(1)}, u32[]{:S(2)}, u32[]{:S(2)}) collective-permute-start(bf16[2,1024,128]{2,1,0:T(8,128)(2,1)S(1)} %slice.77), channel_id=1, source_target_pairs={{0,1},{1,0},{2,3},{3,2},{4,5},{5,4},{6,7},{7,6},{8,9},{9,8},{10,11... | collective-permute-start | bytes 1572872 | tf_op jit(solution)/shard_map/ppermute | solution.py:44
  (20 other events, 65.2 us)
where the time goes:
time: 600 us; the launch traced here: 589 us
  Pallas kernels  520 us (87%)
  other arithmetic  21.5 us (4%)
  local copies, waits for them, and re-layouts  21.4 us (4%)
  starting transfers between devices  21.2 us (4%)
    pallas_call x1, Pallas kernels, middle(): pl.pallas_call(functools.partial(middle_kernel, len(slabs), len(downs), l...  154 us
    pallas_call x1, Pallas kernels, last(): pl.pallas_call(functools.partial(last_kernel, line), out_shape=(shape((ro...  126 us
    pallas_call x1, Pallas kernels, first(): pl.pallas_call(functools.partial(first_kernel, count // 2), out_shape=(sh...  120 us
    pallas_call x2, Pallas kernels, attend_back(): pl.pallas_call(functools.partial(attend_back_kernel, which), out_shape=(s...  82.7 us
    pallas_call x1, Pallas kernels, attend(): pl.pallas_call(attend_kernel, out_shape=(jax.ShapeDtypeStruct((heads, row...  37.3 us
    unnamed x86, local copies, waits for them, and re-layouts  13.4 us
    ppermute x7, starting transfers between devices, swap(): return lax.ppermute(block, axis, [(i, i ^ bit) for i in range(count)])  13.1 us
  transfers between devices with their start and end apart: 13, of which 1 were waited for; matrix products, arithmetic and copies ran while one was open for 2% of the time, Pallas kernels for 20%

commit v1 on v0

--- a/solution.py
+++ b/solution.py
@@ -255,6 +255,7 @@
     start_ref,
     dq_ref,
     low_ref,
+    pair_ref,
     own_ref,
     keys,
     values,
@@ -367,7 +368,8 @@
             part = dkv[source, :]
             part = jnp.where(low_lane, part * SCALE, part)
             if block < BACK:
-                low_ref[(0, 2, 1, 3)[block], tile, :] = part.astype(BF)
+                target = pair_ref if block % 2 else low_ref
+                target[block // 2, tile, :] = part.astype(BF)
             else:
                 own_ref[tile, :] = part
         return carry
@@ -385,11 +387,12 @@
         functools.partial(attend_back_kernel, which),
         out_shape=(
             shape((rows, count * HEAD), F32),
-            shape((BACK, rows, 128), BF),
+            shape((BACK // 2, rows, 128), BF),
+            shape((BACK // 2, rows, 128), BF),
             shape((rows, 128), F32),
         ),
         in_specs=[pl.BlockSpec(memory_space=pltpu.SMEM)] + [vmem] * 6,
-        out_specs=(vmem,) * 3,
+        out_specs=(vmem,) * 4,
         scratch_shapes=[
             pltpu.VMEM((window, 256), BF),
             pltpu.VMEM((window, 128), BF),
@@ -540,8 +543,6 @@
     slab_on = [
         remote(SLAB + h, slab_refs[-1].at[h], slab_at(h, last), (me, after)) for h in range(4)
     ]
-    for copy in slab_on:
-        copy.start()
     load_slabs = [
         local(7 + 4 * i + h, ref.at[h], slab_at(h, (place + line - i) % line))
         for i, ref in enumerate(slab_refs)
@@ -564,7 +565,7 @@
             for i, ref in enumerate(down_refs)
         ]
         down_last = [remote(DOWN_LAST, down_refs[-1], down_at(last), (me, after))]
-    for copy in down_last:
+    for copy in down_last + slab_on:
         copy.start()
     slot = side * 4 + me
     far_slot, across_slot = side * 4 + beside, (1 - side) * 4 + me
@@ -629,6 +630,23 @@
     near.start()
     far.start()
     across.start()
+    for copy in load_down + load_top + [keep_weight]:
+        copy.wait()
+    for copy in down_last + top_on:
+        copy.wait_recv()
+
+    def hidden_back(step, carry):
+        for first, size in SPANS:
+            grad = nt(
+                tops[pl.ds(2 * step, 2)].reshape(2 * rows, width),
+                w_dn[first : first + size, :],
+            )
+            grad_gu[pl.ds(2 * step, 2), :, units + first : units + first + size] = (
+                grad.astype(BF).reshape(2, rows, size)
+            )
+        return carry
+
+    lax.fori_loop(0, 4, hidden_back, 0)
     far.wait_recv()
     far_on.start()
     corner_top.start()
@@ -637,11 +655,7 @@
     corner_low.start()
     for copy in load_slabs:
         copy.wait()
-    for copy in slab_on + down_last:
-        copy.wait_recv()
-    for copy in load_down + load_top + [keep_weight]:
-        copy.wait()
-    for copy in top_on:
+    for copy in slab_on:
         copy.wait_recv()
 
     def pair_rows(index, first=0, size=rows):
@@ -686,9 +700,8 @@
             block = acts[pl.ds(pair, 2)].reshape(2 * rows, width)
             gate = nn(block, w_gu[:, first : first + size])
             up = nn(block, w_gu[:, units + first : units + first + size])
-            grad = nt(
-                tops[pl.ds(pair, 2)].reshape(2 * rows, width), w_dn[first : first + size, :]
-            )
+            grad = grad_gu[pl.ds(pair, 2), :, units + first : units + first + size]
+            grad = grad.reshape(2 * rows, size).astype(F32)
             sig = jax.nn.sigmoid(gate)
             silu = gate * sig
             shape = (2, rows, size)
@@ -1028,7 +1041,7 @@
 TOK_NEAR, TOK_FAR, TOK_ON, IN_QUERY, IN_REST = 0, 1, 2, 3, 6
 TOP_FAR = 9
 UNITS_MOVE, SLAB_ON, DOWN_ON = 11, 18, 19
-KV_ONE, KV_TWO, KV_PAIR_ONE, KV_PAIR_TWO, FIRST_TRANSFERS = 20, 21, 22, 23, 24
+KV_ONE, KV_TWO, KV_PAIR_ONE, KV_PAIR_TWO, FIRST_TRANSFERS = 20, 22, 24, 26, 28
 COLS_Q = QHEADS // 4 * HEAD
 COLS_IN = COLS_Q + 4 * HEAD
 
@@ -1272,22 +1285,34 @@
     keep_toks = local(16, toks, toks_out)
     keep_toks.start()
 
-    def project(step, carry):
-        tile = pl.ds(pl.multiple_of(step * 256, 256), 256)
-        for first, size in SPANS:
-            weight = w_in[:, :, :, first : first + size].reshape(width, size)
-            raw[tile, first : first + size] = nn(normed[tile, :], weight)
-        return carry
-
-    lax.fori_loop(0, 4 * rows // 256, project, 0)
-    keep_raw = local(12, raw.at[:, pl.ds(0, COLS_Q + 128)], raw_out)
-    keep_raw.start()
+    def project(spans):
+        def tile_of(step, carry):
+            tile = pl.ds(pl.multiple_of(step * 256, 256), 256)
+            for first, size in spans:
+                weight = w_in[:, :, :, first : first + size].reshape(width, size)
+                raw[tile, first : first + size] = nn(normed[tile, :], weight)
+            return carry
+
+        lax.fori_loop(0, 4 * rows // 256, tile_of, 0)
 
     def rotated(block, gain, tile):
         block = block * head_scale(block) * gain
         return block * cos_ref[tile, :] + swap_halves(block) * sin_ref[tile, :]
 
-    def prepare(step, carry):
+    def prepare_keys(step, carry):
+        tile = pl.ds(pl.multiple_of(step * 64, 64), 64)
+        first_half = lanes((64, 128)) < HEAD
+        keys = rotated(raw[tile, COLS_Q : COLS_Q + 128], key_gain_ref[...], tile)
+        values = raw[tile, COLS_Q + 128 : COLS_Q + 256]
+        kv_own[0, tile, :] = jnp.where(
+            first_half, keys, pltpu.roll(values, HEAD, 1)
+        ).astype(BF)
+        kv_own[1, tile, :] = jnp.where(
+            first_half, pltpu.roll(keys, HEAD, 1), values
+        ).astype(BF)
+        return carry
+
+    def prepare_queries(step, carry):
         tile = pl.ds(pl.multiple_of(step * 64, 64), 64)
         first_half = lanes((64, 128)) < HEAD
         for t in range(QHEADS // 4 // 2):
@@ -1305,30 +1330,50 @@
             wide[2 * t + 1, tile, :] = jnp.where(
                 first_half, pltpu.roll(upper, HEAD, 1), lower
             ).astype(BF)
-        keys = rotated(raw[tile, COLS_Q : COLS_Q + 128], key_gain_ref[...], tile)
-        values = raw[tile, COLS_Q + 128 : COLS_Q + 256]
-        kv_own[0, tile, :] = jnp.where(
-            first_half, keys, pltpu.roll(values, HEAD, 1)
-        ).astype(BF)
-        kv_own[1, tile, :] = jnp.where(
-            first_half, pltpu.roll(keys, HEAD, 1), values
-        ).astype(BF)
-        return carry
-
-    lax.fori_loop(0, 4 * rows // 64, prepare, 0)
-
-    kv_one = remote(KV_ONE, kv_own, kv_out.at[2], (me, after))
-    kv_two = remote(KV_TWO, kv_out.at[2], kv_out.at[0], (me, after))
-    pair_one_even = remote(KV_PAIR_ONE, kv_own, kv_out.at[3], (me, other))
-    pair_one_odd = remote(KV_PAIR_ONE, kv_out.at[2], kv_out.at[3], (me, other))
-    pair_two_even = remote(KV_PAIR_TWO, kv_out.at[2], kv_out.at[1], (me, other))
-    pair_two_odd = remote(KV_PAIR_TWO, kv_out.at[0], kv_out.at[1], (me, other))
-    kv_one.start()
+        return carry
+
+    project(((COLS_Q, 256),))
+    lax.fori_loop(0, 4 * rows // 64, prepare_keys, 0)
+
+    def kv_copies(index, source, target, device):
+        return [remote(index + g, source(g), kv_out.at[target, g], device) for g in (0, 1)]
+
+    def kv_from(block):
+        return lambda g: kv_out.at[block, g]
+
+    def kv_mine(g):
+        return kv_own.at[g]
+
+    kv_one = kv_copies(KV_ONE, kv_mine, 2, (me, after))
+    kv_two = kv_copies(KV_TWO, kv_from(2), 0, (me, after))
+    pair_one_even = kv_copies(KV_PAIR_ONE, kv_mine, 3, (me, other))
+    pair_one_odd = kv_copies(KV_PAIR_ONE, kv_from(2), 3, (me, other))
+    pair_two_even = kv_copies(KV_PAIR_TWO, kv_from(2), 1, (me, other))
+    pair_two_odd = kv_copies(KV_PAIR_TWO, kv_from(0), 1, (me, other))
+    for g in (0, 1):
+        kv_one[g].start()
 
     @pl.when(side == 0)
     def _():
-        pair_one_even.start()
-
+        for g in (0, 1):
+            pair_one_even[g].start()
+
+    project(((0, 256), (256, 128)))
+    keep_raw = local(12, raw.at[:, pl.ds(0, COLS_Q + 128)], raw_out)
+    keep_raw.start()
+    for g in (0, 1):
+        kv_one[g].wait_recv()
+        kv_two[g].start()
+
+        @pl.when(side == 0)
+        def _(g=g):
+            pair_two_even[g].start()
+
+        @pl.when(side == 1)
+        def _(g=g):
+            pair_one_odd[g].start()
+
+    lax.fori_loop(0, 4 * rows // 64, prepare_queries, 0)
     keep = [
         local(13, kv_own, kv_out.at[4]),
         local(14, wide, wide_out),
@@ -1336,25 +1381,16 @@
     ]
     for copy in keep:
         copy.start()
-    kv_one.wait_recv()
-    kv_two.start()
-
-    @pl.when(side == 0)
-    def _():
-        pair_two_even.start()
-
-    @pl.when(side == 1)
-    def _():
-        pair_one_odd.start()
-
-    kv_two.wait_recv()
-
-    @pl.when(side == 1)
-    def _():
-        pair_two_odd.start()
-
-    pair_one_even.wait_recv()
-    pair_two_even.wait_recv()
+    for g in (0, 1):
+        kv_two[g].wait_recv()
+
+        @pl.when(side == 1)
+        def _(g=g):
+            pair_two_odd[g].start()
+
+    for g in (0, 1):
+        pair_one_even[g].wait_recv()
+        pair_two_even[g].wait_recv()
     down_on.wait_recv()
     slab_on.wait_recv()
     top_far.wait_recv()
@@ -1364,10 +1400,8 @@
         copy.wait_send()
     for copy in (tok_near, tok_far, tok_on, top_far):
         copy.wait_send()
-    for copy in (slab_on, down_on, kv_one, kv_two):
+    for copy in [slab_on, down_on] + kv_one + kv_two + pair_one_even + pair_two_even:
         copy.wait_send()
-    pair_one_even.wait_send()
-    pair_two_even.wait_send()
 
     for step in range(line):
         swap_copy(step).wait_send()
@@ -1514,6 +1548,7 @@
     dq_two_ref,
     low_four_ref,
     low_two_ref,
+    pair_two_ref,
     own_four_ref,
     own_two_ref,
     pair_four_ref,
@@ -1627,11 +1662,11 @@
 
     units_own_part = parts.at[:, pl.ds(0, 2 * w_rows), pl.ds(0, units_ref.shape[2])]
     low_refs, own_refs = (low_four_ref, low_two_ref), (own_four_ref, own_two_ref)
-    three_on = remote(THREE, low_refs[1].at[2], three.at[1], (me, other))
-    one_on = remote(ONE, low_refs[1].at[3], one.at[1], (me, other))
+    three_on = remote(THREE, pair_two_ref.at[0], three.at[1], (me, other))
+    one_on = remote(ONE, pair_two_ref.at[1], one.at[1], (me, other))
     three_on.start()
     one_on.start()
-    low_loads = [local(6 + g, low_refs[g].at[pl.ds(0, 2)], low.at[g]) for g in (0, 1)]
+    low_loads = [local(6 + g, low_refs[g], low.at[g]) for g in (0, 1)]
     pair_loads = [
         local(11, pair_four_ref.at[0], three.at[0]),
         local(12, pair_four_ref.at[1], one.at[0]),
@@ -1677,9 +1712,9 @@
         return LineSum(part, got, hold, arrive, sems, places, remote)
 
     query_line = line_sum(
-        0, lambda b: query_part.at[:, b], query_got, query_hold, query_arrive
+        0, lambda b: query_part.at[b], query_got, query_hold, query_arrive
     )
-    rest_line = line_sum(1, lambda b: rest_part.at[:, b], rest_got, rest_hold, rest_arrive)
+    rest_line = line_sum(1, lambda b: rest_part.at[b], rest_got, rest_hold, rest_arrive)
     slab_line = line_sum(2, lambda b: slab.at[b], slab_got, slab_hold, slab_arrive)
 
     four_on = [remote(FOUR_ON + g, low.at[g, 0], four_in.at[g], (me, before)) for g in (0, 1)]
@@ -1713,6 +1748,22 @@
     for copy in low_loads + pair_loads:
         copy.wait()
     add_pair(0)
+    loads[8].wait()
+    loads[9].wait()
+
+    def add_units(step, carry):
+        head, tile = step // (2 * w_rows // 16), step % (2 * w_rows // 16)
+        tile = pl.ds(pl.multiple_of(tile * 16, 16), 16)
+        total = units_sum[head, tile, :].astype(F32) + units_own_part[head, tile, :].astype(F32)
+        units_sum[head, tile, :] = total.astype(BF)
+        return carry
+
+    lax.fori_loop(0, 8 * w_rows // 16, add_units, 0)
+    for copy in homes:
+        copy.start()
+    units_own.start()
+    loads[4].wait()
+    slab_line.start()
 
     head_gains[...] = jnp.zeros_like(head_gains)
     gain_rows[...] = jnp.zeros_like(gain_rows)
@@ -1755,7 +1806,7 @@
         turned[span, :] = transposed(normed[:, span])
         first = pl.ds(step % tiles_per_head * per_tile, per_tile)
         part = nn(turned[span, :], grads[:, 0:COLS_Q])
-        query_part[step // tiles_per_head, first] = part.astype(BF).reshape(
+        query_part[first, step // tiles_per_head] = part.astype(BF).reshape(
             per_tile, w_rows, COLS_Q
         )
         return carry
@@ -1763,8 +1814,7 @@
     lax.fori_loop(0, width // 256, query_weights, 0)
     query_line.start()
     add_four(1)
-    loads[4].wait()
-    slab_line.start()
+    slab_line.step(1)
 
     loads[3].wait()
 
@@ -1789,17 +1839,6 @@
 
     lax.fori_loop(0, width // 256, add_down, 0)
     down_last.start()
-    loads[8].wait()
-    loads[9].wait()
-
-    def add_units(step, carry):
-        head, tile = step // (2 * w_rows // 16), step % (2 * w_rows // 16)
-        tile = pl.ds(pl.multiple_of(tile * 16, 16), 16)
-        total = units_sum[head, tile, :].astype(F32) + units_own_part[head, tile, :].astype(F32)
-        units_sum[head, tile, :] = total.astype(BF)
-        return carry
-
-    lax.fori_loop(0, 8 * w_rows // 16, add_units, 0)
     query_line.step(1)
     for copy in two_on:
         copy.wait_recv()
@@ -1822,6 +1861,18 @@
 
     lax.fori_loop(0, block // 64, key_rows, 0)
 
+    def gain_round(i):
+        return remote(i, head_gains.at[i], gains_in.at[i], rounds[i], gain_sends, gain_recvs)
+
+    def gain_step(i):
+        if 0 <= i < len(rounds):
+            gain_round(i).wait_recv()
+            head_gains[i + 1] = head_gains[i] + gains_in[i]
+        if i + 1 < len(rounds):
+            gain_round(i + 1).start()
+
+    gain_step(-1)
+
     loads[2].wait()
 
     def token_cols(step, carry):
@@ -1848,18 +1899,41 @@
         first = pl.ds(step % tiles_per_head * per_tile, per_tile)
         head = step // tiles_per_head
         part = nn(turned[span, :], grads[:, COLS_Q : COLS_Q + 256])
-        rest_part[head, first, :, 0:256] = part.astype(BF).reshape(per_tile, w_rows, 256)
+        rest_part[first, head, :, 0:256] = part.astype(BF).reshape(per_tile, w_rows, 256)
         gain_cols = transposed(gain_rows[:, span])
-        rest_part[head, first, :, 256:384] = gain_cols.astype(BF).reshape(per_tile, w_rows, 128)
+        rest_part[first, head, :, 256:384] = gain_cols.astype(BF).reshape(per_tile, w_rows, 128)
         return carry
 
     lax.fori_loop(0, width // 256, rest_weights, 0)
     rest_line.start()
-    for copy in homes:
-        copy.start()
-    units_own.start()
-    slab_line.step(1)
-    for step in range(2, line + 1):
+    gain_step(0)
+    to_mate[0].wait_recv()
+
+    def add_part(step, carry):
+        tile = pl.ds(pl.multiple_of(step * 32, 32), 32)
+        parts[beside, tile, :] = (
+            parts[beside, tile, :].astype(F32) + part_got[1, tile, :].astype(F32)
+        ).astype(BF)
+        return carry
+
+    lax.fori_loop(0, rows // 32, add_part, 0)
+    part_on = remote(PART_FAR, parts.at[beside], part_far, (beside, at))
+    part_on.start()
+
+    query_line.step(2, query_sum)
+    slab_line.step(2, w_out_out)
+
+    loads[6].wait()
+    down_last.wait_recv()
+
+    def down_rows(step, carry):
+        span = pl.ds(pl.multiple_of(step * 256, 256), 256)
+        down_out[:, span] = down_own[1, :, span].astype(F32) + down_in[1, :, span].astype(F32)
+        return carry
+
+    lax.fori_loop(0, width // 256, down_rows, 0)
+    gain_step(1)
+    for step in range(3, line + 1):
         query_line.step(step, query_sum)
     query_home = [
         remote(QUERY_HOME + i, query_sum.at[to], query_in.at[me], (to, at))
@@ -1869,72 +1943,6 @@
     for copy in query_home:
         copy.start()
     query_own.start()
-    to_mate[0].wait_recv()
-
-    def add_part(step, carry):
-        tile = pl.ds(pl.multiple_of(step * 32, 32), 32)
-        parts[beside, tile, :] = (
-            parts[beside, tile, :].astype(F32) + part_got[1, tile, :].astype(F32)
-        ).astype(BF)
-        return carry
-
-    lax.fori_loop(0, rows // 32, add_part, 0)
-    part_on = remote(PART_FAR, parts.at[beside], part_far, (beside, at))
-    part_on.start()
-
-    def gain_round(i):
-        return remote(i, head_gains.at[i], gains_in.at[i], rounds[i], gain_sends, gain_recvs)
-
-    rest_line.step(1)
-    for i in range(len(rounds)):
-        gain_round(i).start()
-        gain_round(i).wait_recv()
-        head_gains[i + 1] = head_gains[i] + gains_in[i]
-        if i + 2 <= line:
-            slab_line.step(i + 2, w_out_out)
-            rest_line.step(i + 2, rest_sum)
-    for step in range(len(rounds) + 2, line + 1):
-        slab_line.step(step, w_out_out)
-        rest_line.step(step, rest_sum)
-    gains_out[...] = head_gains[len(rounds)]
-    rest_home = [
-        remote(REST_HOME + i, rest_sum.at[to], rest_in.at[me], (to, at))
-        for i, to in enumerate((mate, beside, corner))
-    ]
-    rest_own = local(14, rest_sum.at[me], rest_in.at[me])
-    for copy in rest_home:
-        copy.start()
-    rest_own.start()
-
-    to_mate[1].wait_recv()
-    part_on.wait_recv()
-    loads[7].wait()
-
-    def norm_back(step, carry):
-        tile = pl.ds(pl.multiple_of(step * 32, 32), 32)
-        grad = (
-            parts[me, tile, :].astype(F32)
-            + part_got[0, tile, :].astype(F32)
-            + part_far[tile, :].astype(F32)
-        )
-        value = toks[me, tile, :].astype(F32)
-        scale = lax.rsqrt(jnp.mean(value * value, axis=1, keepdims=True) + EPS)
-        inner = grad * gain_ref[0:1, :]
-        mean = jnp.mean(inner * value, axis=1, keepdims=True)
-        dx_out[tile, :] += scale * inner - value * (scale * scale * scale * mean)
-        return carry
-
-    lax.fori_loop(0, rows // 32, norm_back, 0)
-
-    loads[6].wait()
-    down_last.wait_recv()
-
-    def down_rows(step, carry):
-        span = pl.ds(pl.multiple_of(step * 256, 256), 256)
-        down_out[:, span] = down_own[1, :, span].astype(F32) + down_in[1, :, span].astype(F32)
-        return carry
-
-    lax.fori_loop(0, width // 256, down_rows, 0)
     for copy in homes:
         copy.wait()
     units_own.wait()
@@ -1951,6 +1959,45 @@
                 for p in range(2 * line)
             ]
             out[:, 2 * units * head : 2 * units * (head + 1)] = jnp.concatenate(pieces, axis=1)
+    gain_step(2)
+    rest_line.step(1)
+    for step in range(2, line + 1):
+        if step > 2:
+            slab_line.step(step, w_out_out)
+        rest_line.step(step, rest_sum)
+        gain_step(step + 1)
+    rest_home = [
+        remote(REST_HOME + i, rest_sum.at[to], rest_in.at[me], (to, at))
+        for i, to in enumerate((mate, beside, corner))
+    ]
+    rest_own = local(14, rest_sum.at[me], rest_in.at[me])
+    for copy in rest_home:
+        copy.start()
+    rest_own.start()
+    for i in range(line + 2, len(rounds)):
+        gain_step(i)
+    gains_out[...] = head_gains[len(rounds)]
+
+    to_mate[1].wait_recv()
+    part_on.wait_recv()
+    loads[7].wait()
+
+    def norm_back(step, carry):
+        tile = pl.ds(pl.multiple_of(step * 32, 32), 32)
+        grad = (
+            parts[me, tile, :].astype(F32)
+            + part_got[0, tile, :].astype(F32)
+            + part_far[tile, :].astype(F32)
+        )
+        value = toks[me, tile, :].astype(F32)
+        scale = lax.rsqrt(jnp.mean(value * value, axis=1, keepdims=True) + EPS)
+        inner = grad * gain_ref[0:1, :]
+        mean = jnp.mean(inner * value, axis=1, keepdims=True)
+        dx_out[tile, :] += scale * inner - value * (scale * scale * scale * mean)
+        return carry
+
+    lax.fori_loop(0, rows // 32, norm_back, 0)
+
     for copy in query_home:
         copy.wait()
     query_own.wait()
@@ -1983,7 +2030,7 @@
 
 
 def last(
-    dq, dkv_low, dkv_own, pair_four, raw, cosine, sine, query_gain, key_gain, normed, w_in, toks,
+    dq, dkv_low, pair_two, dkv_own, pair_four, raw, cosine, sine, query_gain, key_gain, normed, w_in, toks,
     gains, gain_two, units, units_parts, down, down_parts, slab, grad,
 ):
     _, rows, width = toks.shape
@@ -2011,7 +2058,7 @@
             shape((out_rows, width), F32),
             shape((8, 128), F32),
         ),
-        in_specs=[vmem] * 2 + [anywhere] * 2 + [vmem] * 2 + [anywhere] * 2 + [vmem] * 4
+        in_specs=[vmem] * 2 + [anywhere] * 3 + [vmem] * 2 + [anywhere] * 2 + [vmem] * 4
         + [anywhere] * 3 + [vmem] * 2 + [anywhere] * 6,
         out_specs=(vmem,) * 10,
         scratch_shapes=[
@@ -2027,8 +2074,8 @@
             pltpu.VMEM(toks.shape, BF),
             pltpu.VMEM((block, 1), F32),
             pltpu.VMEM((block, COLS_IN), BF),
-            pltpu.VMEM((4, count, w_rows, COLS_Q), BF),
-            pltpu.VMEM((4, count, w_rows, COLS_Q), BF),
+            pltpu.VMEM((count, 4, w_rows, COLS_Q), BF),
+            pltpu.VMEM((count, 4, w_rows, COLS_Q), BF),
             pltpu.VMEM((line,) + part, BF),
             pltpu.VMEM((line,) + part, BF),
             pltpu.VMEM((line - 1,) + part, BF),
@@ -2068,7 +2115,7 @@
         ),
         name="last",
     )(
-        *dq, *dkv_low, *dkv_own, pair_four, raw, cosine, sine, query_gain, key_gain, normed, w_in,
+        *dq, *dkv_low, pair_two, *dkv_own, pair_four, raw, cosine, sine, query_gain, key_gain, normed, w_in,
         toks, gains, gain_two, units, units_parts, down, down_parts, slab, grad,
     )
 
@@ -2255,7 +2302,7 @@
     down_sum.add()
     gu_sum.add()
     gu_moved = gu_sum.send()
-    pair_four = swap(four[1][2:], "blk", 1)
+    pair_four = swap(four[2], "blk", 1)
     slab_far = swap((weight_own[1].astype(F32) + weight_in[1].astype(F32)).astype(BF), "head", 2)
     two = back(1, kv=kv_window)
     four, two, gu_moved, pair_four, slab_far = sync(four, two, gu_moved, pair_four, slab_far)
@@ -2282,7 +2329,8 @@
     ) = last(
         (four[0], two[0]),
         (four[1], two[1]),
-        (four[2], two[2]),
+        two[2],
+        (four[3], two[3]),
         pair_four,
         raw,
         cosine,

time: 600 us -> 581 us (0.968)
  the two profiles are of different devices: /device:TPU:17 before, /device:TPU:0 now
where the time goes in v1:
time: 581 us; the launch traced here: 585 us
  Pallas kernels  472 us (81%)
  waiting for transfers between devices  48.3 us (8%)
  local copies, waits for them, and re-layouts  22.1 us (4%)
  starting transfers between devices  22.1 us (4%)
  other arithmetic  19 us (3%)
    pallas_call x1, Pallas kernels, middle(): pl.pallas_call(functools.partial(middle_kernel, len(slabs), len(downs), l...  156 us
    pallas_call x1, Pallas kernels, last(): pl.pallas_call(functools.partial(last_kernel, line), out_shape=(shape((ro...  144 us
    pallas_call x1, Pallas kernels, first(): pl.pallas_call(functools.partial(first_kernel, count // 2), out_shape=(sh...  121 us
    pallas_call x2, Pallas kernels, attend_back(): pl.pallas_call(functools.partial(attend_back_kernel, which), out_shape=(s...  35.9 us
    ppermute x7, waiting for transfers between devices, swap(): return lax.ppermute(block, axis, [(i, i ^ bit) for i in range(count)])  26 us
    ppermute x5, waiting for transfers between devices, ring(): lax.ppermute(block, 'blk', [(i, (i + step) % count) for i in range(count)])  17.8 us
    pallas_call x1, Pallas kernels, attend(): pl.pallas_call(attend_kernel, out_shape=(jax.ShapeDtypeStruct((heads, row...  15.8 us
    ppermute x7, starting transfers between devices, swap(): return lax.ppermute(block, axis, [(i, i ^ bit) for i in range(count)])  14.5 us
  transfers between devices with their start and end apart: 13, of which 5 were waited for; matrix products, arithmetic and copies ran while one was open for 2% of the time, Pallas kernels for 9%

profile of v1, /device:TPU:0, one launch (start us, length us, event | category | flops | bytes accessed | tf_op | source)
XLA Modules:
  0.0 585.3 jit_solution(15634102500226115345)
XLA Ops:
  5.0 1.9 fusion.5
  8.0 120.7 %first.1 = (bf16[6,1024,128]{2,1,0:T(8,128)(2,1)}, bf16[6,1024,128]{2,1,0:T(8,128)(2,1)}, bf16[5,2,1024,128]{3,2,1,0:T(8,128)(2,1)}, f32[1024,512]{1,0:T(8,128)}...) custom-call(bf16[256,2048]{1,0:T(8,128)(2,1)} %tokens_ref.3, ...), custom_call_target="tpu_custom_call" | custom-call | flops 60000002048 | bytes 60000000 | tf_op jit(solution)/shard_map/first/pallas_call | solution.py:1428
  128.8 1.0 collective-permute-start
  129.8 2.3 collective-permute-start.1
  132.6 2.0 collective-permute-start.4
  135.4 1.7 copy-done.14
  137.1 1.4 copy-done.15
  138.5 15.8 %attend.1 = (f32[6,1024,128]{2,1,0:T(8,128)}, bf16[1024,384]{1,0:T(8,128)(2,1)S(1)}) custom-call(s32[9]{0:T(128)S(1)} %pad_add_fusion.1.meta_ref, bf16[6,1024,128]{2,1,0:T(8,128)(2,1)S(1)} %copy-done.15, bf16[5,2,1024,128]{3,2,1,0:T(8,128)(2,1)S(1)} %copy-done.14, s32[1024,1]{1,0:T(8,128)S(1)} %copy.72.start_ref), custom_call_target="tpu_custom_call" | custom-call | flops 60000002048 | bytes 20000000 | tf_op jit(solution)/shard_map/attend/pallas_call | solution.py:226
  155.8 17.8 %collective-permute-done.1.refs_5_ = bf16[160,2048]{1,0:T(8,128)(2,1)} collective-permute-done((bf16[160,2048]{1,0:T(8,128)(2,1)S(1)}, bf16[160,2048]{1,0:T(8,128)(2,1)}, u32[]{:S(2)}, u32[]{:S(2)}) %collective-permute-start.1) | collective-permute-done | bytes 655392 | tf_op jit(solution)/shard_map/ppermute | solution.py:49
  173.5 3.5 collective-permute-done.4.top_corner_ref
  177.1 156.0 %middle.1 = (f32[256,2048]{1,0:T(8,128)}, f32[256,2048]{1,0:T(8,128)}, bf16[256,2048]{1,0:T(8,128)(2,1)}, bf16[256,1536]{1,0:T(8,128)(2,1)}, bf16[4,256,384]{2,1...) custom-call(bf16[4,256,384]{2,1,0:T(8,128)(2,1)} %bitcast.52, ...), custom_call_target="tpu_custom_call" | custom-call | flops 60000002048 | bytes 100000000 | tf_op jit(solution)/shard_map/middle/pallas_call | solution.py:984
  333.1 2.1 dynamic-slice_bitcast_fusion
  335.6 2.9 fusion.2
  339.0 1.6 collective-permute-start.8
  340.6 1.4 collective-permute-start.9
  342.0 21.1 %attend_back_four.1 = (f32[1024,256]{1,0:T(8,128)S(1)}, bf16[2,1024,128]{2,1,0:T(8,128)(2,1)S(1)}, bf16[2,1024,128]{2,1,0:T(8,128)(2,1)S(1)}, f32[1024,128]{1,0:T(8,128)S(1)}) custom-call(s32[9]{0:T(128)S(1)} %pad_add_fusion.1.meta_ref, bf16[6,1024,128]{2,1,0:T(8,128)(2,1)S(1)} %copy-done.16, bf16[6,1024,128]{2,1,0:T(8,128)(2,1)} %get-tuple-element.128.query_ref, ...), custom_call_target="tpu_custom_call" | custom-call | flops 80000000000 | bytes 40000000 | tf_op jit(solution)/shard_map/attend_back_four/pallas_call | solution.py:386
  364.9 17.8 %collective-permute-done.8 = bf16[256,2048]{1,0:T(8,128)(2,1)} collective-permute-done((bf16[256,2048]{1,0:T(8,128)(2,1)}, bf16[256,2048]{1,0:T(8,128)(2,1)}, u32[]{:S(2)}, u32[]{:S(2)}) %collective-permute-start.8) | collective-permute-done | bytes 1048608 | tf_op jit(solution)/shard_map/ppermute | solution.py:44
  382.8 4.6 collective-permute-done.9
  387.4 1.6 fusion.1
  389.0 2.5 collective-permute-start.10
  391.6 14.8 %attend_back_two.1 = (f32[1024,128]{1,0:T(8,128)S(1)}, bf16[2,1024,128]{2,1,0:T(8,128)(2,1)S(1)}, bf16[2,1024,128]{2,1,0:T(8,128)(2,1)S(1)}, f32[1024,128]{1,0:T(8,128)S(1)}) custom-call(s32[9]{0:T(128)S(1)} %pad_add_fusion.1.meta_ref, bf16[6,1024,128]{2,1,0:T(8,128)(2,1)S(1)} %copy-done.16, bf16[6,1024,128]{2,1,0:T(8,128)(2,1)S(1)} %copy-done.17, ...), custom_call_target="tpu_custom_call" | custom-call | flops 40000000000 | bytes 40000000 | tf_op jit(solution)/shard_map/attend_back_two/pallas_call | solution.py:386
  406.4 9.3 %collective-permute-start.11 = (bf16[2,1024,128]{2,1,0:T(8,128)(2,1)S(1)}, bf16[2,1024,128]{2,1,0:T(8,128)(2,1)S(1)}, u32[]{:S(2)}, u32[]{:S(2)}) collective-permute-start(bf16[2,1024,128]{2,1,0:T(8,128)(2,1)S(1)} %get-tuple-element.146), channel_id=1, source_target_pairs={{0,1},{1,0},{2,3},{3,2},{4,5},{5,4},{6,7},{7,6},{8,9},{9,8},{10,11... | collective-permute-start | bytes 1572872 | tf_op jit(solution)/shard_map/ppermute | solution.py:44
  415.7 4.2 add_convert_fusion.1
  419.9 2.3 fusion.4.down_ref
  422.3 4.6 collective-permute-done.11.pair_four_ref
  426.8 2.0 fusion
  428.8 143.8 %last.1 = (f32[256,2048]{1,0:T(8,128)}, f32[64,1536]{1,0:T(8,128)}, f32[64,384]{1,0:T(8,128)}, f32[64,384]{1,0:T(8,128)}, f32[64,128]{1,0:T(8,128)}, /*index=5*/...) custom-call(f32[1024,256]{1,0:T(8,128)} %copy-done.18, ...), custom_call_target="tpu_custom_call" | custom-call | flops 60000002048 | bytes 60000000 | tf_op jit(solution)/shard_map/last/pallas_call | solution.py:2047
  572.7 1.5 slice_reduce_fusion
  575.6 3.3 copy.86
  581.6 1.1 copy.91
  582.7 1.1 copy.92
  583.8 1.1 copy.93
  (123 shorter events, 14.9 us)
Async XLA Ops:
  7.0 121.7 %copy-start.3 = (f32[1,128]{1,0:T(1,128)}, f32[1,128]{1,0:T(1,128)S(1)}, u32[]{:S(2)}) copy-start(f32[1,128]{1,0:T(1,128)S(1)} %get-tuple-element.206.query_gain_ref) | copy-start | bytes 1540
  7.0 121.7 %copy-start.4 = (f32[1,128]{1,0:T(1,128)}, f32[1,128]{1,0:T(1,128)S(1)}, u32[]{:S(2)}) copy-start(f32[1,128]{1,0:T(1,128)S(1)} %get-tuple-element.207.key_gain_ref) | copy-start | bytes 1540
  7.9 120.8 %copy-start = (f32[1024,128]{1,0:T(8,128)}, f32[1024,128]{1,0:T(8,128)S(1)}, u32[]{:S(2)}) copy-start(f32[1024,128]{1,0:T(8,128)S(1)} %get-tuple-element.204.cos_ref) | copy-start | bytes 1572868
  7.9 120.8 %copy-start.1 = (f32[1024,128]{1,0:T(8,128)}, f32[1024,128]{1,0:T(8,128)S(1)}, u32[]{:S(2)}) copy-start(f32[1024,128]{1,0:T(8,128)S(1)} %get-tuple-element.205.sin_ref) | copy-start | bytes 1572868
  8.0 124.7 %copy-start.39 = (bf16[256,2048]{1,0:T(8,128)(2,1)S(1)}, bf16[256,2048]{1,0:T(8,128)(2,1)}, u32[]{:S(2)}) copy-start(bf16[256,2048]{1,0:T(8,128)(2,1)} %top_ref.3) | copy-start | bytes 3145732
  128.7 25.6 %copy-start.5 = (bf16[256,2048]{1,0:T(8,128)(2,1)}, bf16[256,2048]{1,0:T(8,128)(2,1)S(1)}, u32[]{:S(2)}) copy-start(bf16[256,2048]{1,0:T(8,128)(2,1)S(1)} %get-tuple-element.114.top_far_ref) | copy-start | bytes 3145732
  128.7 25.5 %copy-start.9 = (bf16[160,2048]{1,0:T(8,128)(2,1)}, bf16[160,2048]{1,0:T(8,128)(2,1)S(1)}, u32[]{:S(2)}) copy-start(bf16[160,2048]{1,0:T(8,128)(2,1)S(1)} %get-tuple-element.124.refs_4_) | copy-start | bytes 1966084
  128.8 26.4 %copy-start.2 = (f32[8,2048]{1,0:T(8,128)}, f32[8,2048]{1,0:T(8,128)S(1)}, u32[]{:S(2)}) copy-start(f32[8,2048]{1,0:T(8,128)S(1)} %get-tuple-element.117.gain_ref) | copy-start | bytes 196612
  128.8 48.3 %collective-permute-start = (bf16[4,128,1280]{2,1,0:T(8,128)(2,1)}, bf16[4,128,1280]{2,1,0:T(8,128)(2,1)}, u32[]{:S(2)}, u32[]{:S(2)}) collective-permute-start(bf16[4,128,1280]{2,1,0:T(8,128)(2,1)} %get-tuple-element.121.refs_1_), channel_id=1, source_target_pairs={{0,2},{1,3},{2,4},{3,5},{4,6},{5,7},{6,0},{7,1},{8,10},{9,11},{10,... | collective-permute-start | bytes 3932168 | tf_op jit(solution)/shard_map/ppermute | solution.py:49
  129.8 43.8 %collective-permute-start.1 = (bf16[160,2048]{1,0:T(8,128)(2,1)S(1)}, bf16[160,2048]{1,0:T(8,128)(2,1)}, u32[]{:S(2)}, u32[]{:S(2)}) collective-permute-start(bf16[160,2048]{1,0:T(8,128)(2,1)S(1)} %get-tuple-element.124.refs_4_), channel_id=1, source_target_pairs={{0,2},{1,3},{2,4},{3,5},{4,6},{5,7},{6,0},{7,1},{8,10},{9,11},{10,... | collective-permute-start | bytes 1966088 | tf_op jit(solution)/shard_map/ppermute | solution.py:49
  132.1 45.0 %collective-permute-start.2 = (bf16[384,2048]{1,0:T(8,128)(2,1)}, bf16[384,2048]{1,0:T(8,128)(2,1)}, u32[]{:S(2)}, u32[]{:S(2)}) collective-permute-start(bf16[384,2048]{1,0:T(8,128)(2,1)} %bitcast.69), channel_id=1, source_target_pairs={{0,16},{8,24},{16,0},{24,8},{1,17},{9,25},{17,1},{25,9},{2,18},{10... | collective-permute-start | bytes 4718600 | tf_op jit(solution)/shard_map/ppermute | solution.py:44
  132.6 40.9 %collective-permute-start.3 = (bf16[256,2048]{1,0:T(8,128)(2,1)S(1)}, bf16[256,2048]{1,0:T(8,128)(2,1)}, u32[]{:S(2)}, u32[]{:S(2)}) collective-permute-start(bf16[256,2048]{1,0:T(8,128)(2,1)S(1)} %copy-done.39), channel_id=1, source_target_pairs={{0,1},{1,0},{2,3},{3,2},{4,5},{5,4},{6,7},{7,6},{8,9},{9,8},{10,11... | collective-permute-start | bytes 3145736 | tf_op jit(solution)/shard_map/ppermute | solution.py:44
  132.6 44.4 %collective-permute-start.4 = (bf16[256,2048]{1,0:T(8,128)(2,1)S(1)}, bf16[256,2048]{1,0:T(8,128)(2,1)}, u32[]{:S(2)}, u32[]{:S(2)}) collective-permute-start(bf16[256,2048]{1,0:T(8,128)(2,1)S(1)} %get-tuple-element.114.top_far_ref), channel_id=1, source_target_pairs={{0,1},{1,0},{2,3},{3,2},{4,5},{5,4},{6,7},{7,6},{8,9},{9,8},{10,11... | collective-permute-start | bytes 3145736 | tf_op jit(solution)/shard_map/ppermute | solution.py:44
  335.2 6.8 %copy-start.13 = (bf16[4,256,384]{2,1,0:T(8,128)(2,1)S(1)}, bf16[4,256,384]{2,1,0:T(8,128)(2,1)}, u32[]{:S(2)}) copy-start(bf16[4,256,384]{2,1,0:T(8,128)(2,1)} %get-tuple-element.130) | copy-start | bytes 2359300
  335.2 6.8 %copy-start.16 = (bf16[6,1024,128]{2,1,0:T(8,128)(2,1)S(1)}, bf16[6,1024,128]{2,1,0:T(8,128)(2,1)}, u32[]{:S(2)}) copy-start(bf16[6,1024,128]{2,1,0:T(8,128)(2,1)} %get-tuple-element.98.query_ref.wide_ref) | copy-start | bytes 4718596
  335.2 29.2 %collective-permute-start.5 = (bf16[160,2048]{1,0:T(8,128)(2,1)}, bf16[160,2048]{1,0:T(8,128)(2,1)}, u32[]{:S(2)}, u32[]{:S(2)}) collective-permute-start(bf16[160,2048]{1,0:T(8,128)(2,1)} %dynamic-slice_bitcast_fusion), channel_id=1, source_target_pairs={{0,2},{1,3},{2,4},{3,5},{4,6},{5,7},{6,0},{7,1},{8,10},{9,11},{10,... | collective-permute-start | bytes 1966088 | tf_op jit(solution)/shard_map/ppermute | solution.py:49
  338.5 48.9 %collective-permute-start.6 = (bf16[4,128,1280]{2,1,0:T(8,128)(2,1)}, bf16[4,128,1280]{2,1,0:T(8,128)(2,1)S(1)}, u32[]{:S(2)}, u32[]{:S(2)}) collective-permute-start(bf16[4,128,1280]{2,1,0:T(8,128)(2,1)} %fusion.2), channel_id=1, source_target_pairs={{0,2},{1,3},{2,4},{3,5},{4,6},{5,7},{6,0},{7,1},{8,10},{9,11},{10,... | collective-permute-start | bytes 3932168 | tf_op jit(solution)/shard_map/ppermute | solution.py:49
  338.5 26.5 %collective-permute-start.7 = (bf16[256,2048]{1,0:T(8,128)(2,1)}, bf16[256,2048]{1,0:T(8,128)(2,1)}, u32[]{:S(2)}, u32[]{:S(2)}) collective-permute-start(bf16[256,2048]{1,0:T(8,128)(2,1)} %get-tuple-element.138), channel_id=1, source_target_pairs={{0,16},{8,24},{16,0},{24,8},{1,17},{9,25},{17,1},{25,9},{2,18},{10... | collective-permute-start | bytes 3145736 | tf_op jit(solution)/shard_map/ppermute | solution.py:44
  339.0 43.8 %collective-permute-start.8 = (bf16[256,2048]{1,0:T(8,128)(2,1)}, bf16[256,2048]{1,0:T(8,128)(2,1)}, u32[]{:S(2)}, u32[]{:S(2)}) collective-permute-start(bf16[256,2048]{1,0:T(8,128)(2,1)} %get-tuple-element.139), channel_id=1, source_target_pairs={{0,1},{1,0},{2,3},{3,2},{4,5},{5,4},{6,7},{7,6},{8,9},{9,8},{10,11... | collective-permute-start | bytes 3145736 | tf_op jit(solution)/shard_map/ppermute | solution.py:44
  340.6 46.8 %collective-permute-start.9 = (bf16[256,2048]{1,0:T(8,128)(2,1)}, bf16[256,2048]{1,0:T(8,128)(2,1)}, u32[]{:S(2)}, u32[]{:S(2)}) collective-permute-start(bf16[256,2048]{1,0:T(8,128)(2,1)} %get-tuple-element.140), channel_id=1, source_target_pairs={{0,17},{1,16},{2,19},{3,18},{4,21},{5,20},{6,23},{7,22},{8,25},{9,... | collective-permute-start | bytes 3145736 | tf_op jit(solution)/shard_map/ppermute | solution.py:2282
  342.0 21.1 %copy-start.25 = (bf16[2,384,2048]{2,1,0:T(8,128)(2,1)S(1)}, bf16[2,384,2048]{2,1,0:T(8,128)(2,1)}, u32[]{:S(2)}) copy-start(bf16[2,384,2048]{2,1,0:T(8,128)(2,1)} %get-tuple-element.154) | copy-start | bytes 9437188
  342.0 21.1 %copy-start.26 = (bf16[2,384,2048]{2,1,0:T(8,128)(2,1)S(1)}, bf16[2,384,2048]{2,1,0:T(8,128)(2,1)}, u32[]{:S(2)}) copy-start(bf16[2,384,2048]{2,1,0:T(8,128)(2,1)} %get-tuple-element.155) | copy-start | bytes 9437188
  364.4 27.2 %copy-start.17 = (bf16[6,1024,128]{2,1,0:T(8,128)(2,1)S(1)}, bf16[6,1024,128]{2,1,0:T(8,128)(2,1)}, u32[]{:S(2)}) copy-start(bf16[6,1024,128]{2,1,0:T(8,128)(2,1)} %get-tuple-element.128.query_ref) | copy-start | bytes 4718596
  364.4 57.9 %collective-permute-start.12 = (bf16[384,2048]{1,0:T(8,128)(2,1)S(1)}, bf16[384,2048]{1,0:T(8,128)(2,1)S(1)}, u32[]{:S(2)}, u32[]{:S(2)}) collective-permute-start(bf16[384,2048]{1,0:T(8,128)(2,1)S(1)} %fusion.3), channel_id=1, source_target_pairs={{0,16},{8,24},{16,0},{24,8},{1,17},{9,25},{17,1},{25,9},{2,18},{10... | collective-permute-start | bytes 4718600 | tf_op jit(solution)/shard_map/ppermute | solution.py:44
  389.0 26.7 %copy-start.28 = (f32[256,2048]{1,0:T(8,128)S(1)}, f32[256,2048]{1,0:T(8,128)}, u32[]{:S(2)}) copy-start(f32[256,2048]{1,0:T(8,128)} %get-tuple-element.126) | copy-start | bytes 6291460
  389.0 37.8 %collective-permute-start.10 = (bf16[4,128,1280]{2,1,0:T(8,128)(2,1)S(1)}, bf16[4,128,1280]{2,1,0:T(8,128)(2,1)}, u32[]{:S(2)}, u32[]{:S(2)}) collective-permute-start(bf16[4,128,1280]{2,1,0:T(8,128)(2,1)S(1)} %fusion.1), channel_id=1, source_target_pairs={{0,2},{1,3},{2,4},{3,5},{4,6},{5,7},{6,0},{7,1},{8,10},{9,11},{10,... | collective-permute-start | bytes 3932168 | tf_op jit(solution)/shard_map/ppermute | solution.py:49
  406.4 13.5 %copy-start.19 = (f32[1024,128]{1,0:T(8,128)}, f32[1024,128]{1,0:T(8,128)S(1)}, u32[]{:S(2)}) copy-start(f32[1024,128]{1,0:T(8,128)S(1)} %get-tuple-element.157.dq_two_ref) | copy-start | bytes 1572868
  406.4 13.5 %copy-start.20 = (bf16[2,1024,128]{2,1,0:T(8,128)(2,1)}, bf16[2,1024,128]{2,1,0:T(8,128)(2,1)S(1)}, u32[]{:S(2)}) copy-start(bf16[2,1024,128]{2,1,0:T(8,128)(2,1)S(1)} %get-tuple-element.159.low_two_ref) | copy-start | bytes 1572868
  406.4 13.5 %copy-start.21 = (bf16[2,1024,128]{2,1,0:T(8,128)(2,1)}, bf16[2,1024,128]{2,1,0:T(8,128)(2,1)S(1)}, u32[]{:S(2)}) copy-start(bf16[2,1024,128]{2,1,0:T(8,128)(2,1)S(1)} %get-tuple-element.160.pair_two_ref) | copy-start | bytes 1572868
  406.4 13.5 %copy-start.22 = (f32[1024,128]{1,0:T(8,128)}, f32[1024,128]{1,0:T(8,128)S(1)}, u32[]{:S(2)}) copy-start(f32[1024,128]{1,0:T(8,128)S(1)} %get-tuple-element.162.own_two_ref) | copy-start | bytes 1572868
  406.4 20.4 %collective-permute-start.11 = (bf16[2,1024,128]{2,1,0:T(8,128)(2,1)S(1)}, bf16[2,1024,128]{2,1,0:T(8,128)(2,1)S(1)}, u32[]{:S(2)}, u32[]{:S(2)}) collective-permute-start(bf16[2,1024,128]{2,1,0:T(8,128)(2,1)S(1)} %get-tuple-element.146), channel_id=1, source_target_pairs={{0,1},{1,0},{2,3},{3,2},{4,5},{5,4},{6,7},{7,6},{8,9},{9,8},{10,11... | collective-permute-start | bytes 1572872 | tf_op jit(solution)/shard_map/ppermute | solution.py:44
  415.7 11.1 %copy-start.27 = (bf16[2,384,2048]{2,1,0:T(8,128)(2,1)S(1)}, bf16[2,384,2048]{2,1,0:T(8,128)(2,1)}, u32[]{:S(2)}) copy-start(bf16[2,384,2048]{2,1,0:T(8,128)(2,1)} %get-tuple-element.155) | copy-start | bytes 9437188
  (22 other events, 68.1 us)

commit v2 on v1

--- a/solution.py
+++ b/solution.py
@@ -160,7 +160,7 @@
             split_window(kv_ref, keys.at[slot], values.at[slot], step, slot)
         return carry
 
-    lax.fori_loop(0, keys.shape[1] // TILE, fill, 0)
+    lax.fori_loop(meta_ref[1] // TILE, keys.shape[1] // TILE, fill, 0)
     for count, first, slot in head_groups(meta_ref):
         for tile in range(rows // TILE):
             q_at = tile * TILE
@@ -277,10 +277,14 @@
         target = split_window(kv_ref, keys, values, step, slot)
         keys[target, 128:256] = jnp.ones((TILE, 128), BF)
         keys_t[:, target] = transposed(keys[target, 0:128])[0:HEAD, :]
-        dkv[target, :] = jnp.zeros((TILE, 128), F32)
-        return carry
-
-    lax.fori_loop(0, window // TILE, fill, 0)
+        return carry
+
+    def clear_sums(step, carry):
+        dkv[pl.ds(pl.multiple_of(step * TILE, TILE), TILE), :] = jnp.zeros((TILE, 128), F32)
+        return carry
+
+    lax.fori_loop(0, window // TILE, clear_sums, 0)
+    lax.fori_loop(meta_ref[1] // TILE, window // TILE, fill, 0)
 
     def low_terms(value, first):
         out = jnp.zeros_like(value)

time: 581 us -> 572 us (0.985); the launches traced: 585 us -> 563 us
  Pallas kernels: 472 us -> 449 us
  waiting for transfers between devices: 48.3 us -> 56.9 us
  starting transfers between devices: 22.1 us -> 14.6 us
    ppermute x7, waiting for transfers between devices: 26 us -> 35.9 us  [swap(): return lax.ppermute(block, axis, [(i, i ^ bit) for i in range(count)])]
    pallas_call x1, Pallas kernels: 156 us -> 147 us  [middle(): pl.pallas_call(functools.partial(middle_kernel, len(slabs), len(downs), l...]
    pallas_call x1, Pallas kernels: 144 us -> 136 us  [last(): pl.pallas_call(functools.partial(last_kernel, line), out_shape=(shape((ro...]
  transfers between devices with their start and end apart: 13 -> 13, of which waited for: 5 -> 7; matrix products, arithmetic and copies ran while one was open for 2% -> 2% of each run, Pallas kernels for 9% -> 8%
where the time goes in v2:
time: 572 us; the launch traced here: 563 us
  Pallas kernels  449 us (78%)
  waiting for transfers between devices  56.9 us (10%)
  local copies, waits for them, and re-layouts  22.1 us (4%)
  other arithmetic  19 us (3%)
  starting transfers between devices  14.6 us (3%)
    pallas_call x1, Pallas kernels, middle(): pl.pallas_call(functools.partial(middle_kernel, len(slabs), len(downs), l...  147 us
    pallas_call x1, Pallas kernels, last(): pl.pallas_call(functools.partial(last_kernel, line), out_shape=(shape((ro...  136 us
    pallas_call x1, Pallas kernels, first(): pl.pallas_call(functools.partial(first_kernel, count // 2), out_shape=(sh...  121 us
    ppermute x7, waiting for transfers between devices, swap(): return lax.ppermute(block, axis, [(i, i ^ bit) for i in range(count)])  35.9 us
    pallas_call x2, Pallas kernels, attend_back(): pl.pallas_call(functools.partial(attend_back_kernel, which), out_shape=(s...  31.3 us
    ppermute x5, waiting for transfers between devices, ring(): lax.ppermute(block, 'blk', [(i, (i + step) % count) for i in range(count)])  20.6 us
    unnamed x90, local copies, waits for them, and re-layouts  14.1 us
    pallas_call x1, Pallas kernels, attend(): pl.pallas_call(attend_kernel, out_shape=(jax.ShapeDtypeStruct((heads, row...  13.9 us
  transfers between devices with their start and end apart: 13, of which 7 were waited for; matrix products, arithmetic and copies ran while one was open for 2% of the time, Pallas kernels for 8%

profile of v2, /device:TPU:0, one launch (start us, length us, event | category | flops | bytes accessed | tf_op | source)
XLA Modules:
  0.0 563.1 jit_solution(13465323968606944673)
XLA Ops:
  5.0 1.9 fusion.5
  8.0 120.7 %first.1 = (bf16[6,1024,128]{2,1,0:T(8,128)(2,1)}, bf16[6,1024,128]{2,1,0:T(8,128)(2,1)}, bf16[5,2,1024,128]{3,2,1,0:T(8,128)(2,1)}, f32[1024,512]{1,0:T(8,128)}...) custom-call(bf16[256,2048]{1,0:T(8,128)(2,1)} %tokens_ref.3, ...), custom_call_target="tpu_custom_call" | custom-call | flops 60000002048 | bytes 60000000 | tf_op jit(solution)/shard_map/first/pallas_call | solution.py:1432
  128.8 1.0 collective-permute-start
  129.8 2.3 collective-permute-start.1
  132.6 2.0 collective-permute-start.4
  135.4 1.7 copy-done.14
  137.1 1.4 copy-done.15
  138.5 13.9 %attend.1 = (f32[6,1024,128]{2,1,0:T(8,128)}, bf16[1024,384]{1,0:T(8,128)(2,1)S(1)}) custom-call(s32[9]{0:T(128)S(1)} %pad_add_fusion.1.meta_ref, bf16[6,1024,128]{2,1,0:T(8,128)(2,1)S(1)} %copy-done.15, bf16[5,2,1024,128]{3,2,1,0:T(8,128)(2,1)S(1)} %copy-done.14, s32[1024,1]{1,0:T(8,128)S(1)} %copy.72.start_ref), custom_call_target="tpu_custom_call" | custom-call | flops 60000002048 | bytes 20000000 | tf_op jit(solution)/shard_map/attend/pallas_call | solution.py:226
  153.9 19.6 %collective-permute-done.1.refs_5_ = bf16[160,2048]{1,0:T(8,128)(2,1)} collective-permute-done((bf16[160,2048]{1,0:T(8,128)(2,1)S(1)}, bf16[160,2048]{1,0:T(8,128)(2,1)}, u32[]{:S(2)}, u32[]{:S(2)}) %collective-permute-start.1) | collective-permute-done | bytes 655392 | tf_op jit(solution)/shard_map/ppermute | solution.py:49
  173.5 3.5 collective-permute-done.4.top_corner_ref
  177.1 146.7 %middle.1 = (f32[256,2048]{1,0:T(8,128)}, f32[256,2048]{1,0:T(8,128)}, bf16[256,2048]{1,0:T(8,128)(2,1)}, bf16[256,1536]{1,0:T(8,128)(2,1)}, bf16[4,256,384]{2,1...) custom-call(bf16[4,256,384]{2,1,0:T(8,128)(2,1)} %bitcast.52, ...), custom_call_target="tpu_custom_call" | custom-call | flops 60000002048 | bytes 100000000 | tf_op jit(solution)/shard_map/middle/pallas_call | solution.py:988
  323.8 2.1 dynamic-slice_bitcast_fusion
  326.3 2.9 fusion.2
  329.2 1.1 collective-permute-start.7
  331.3 1.4 collective-permute-start.9
  332.7 18.7 %attend_back_four.1 = (f32[1024,256]{1,0:T(8,128)S(1)}, bf16[2,1024,128]{2,1,0:T(8,128)(2,1)S(1)}, bf16[2,1024,128]{2,1,0:T(8,128)(2,1)S(1)}, f32[1024,128]{1,0:T(8,128)S(1)}) custom-call(s32[9]{0:T(128)S(1)} %pad_add_fusion.1.meta_ref, bf16[6,1024,128]{2,1,0:T(8,128)(2,1)S(1)} %copy-done.16, bf16[6,1024,128]{2,1,0:T(8,128)(2,1)} %get-tuple-element.128.query_ref, ...), custom_call_target="tpu_custom_call" | custom-call | flops 80000000000 | bytes 40000000 | tf_op jit(solution)/shard_map/attend_back_four/pallas_call | solution.py:390
  352.8 1.1 collective-permute-start.12
  353.9 1.5 collective-permute-done.7
  355.5 22.5 %collective-permute-done.8 = bf16[256,2048]{1,0:T(8,128)(2,1)} collective-permute-done((bf16[256,2048]{1,0:T(8,128)(2,1)}, bf16[256,2048]{1,0:T(8,128)(2,1)}, u32[]{:S(2)}, u32[]{:S(2)}) %collective-permute-start.8) | collective-permute-done | bytes 1048608 | tf_op jit(solution)/shard_map/ppermute | solution.py:44
  378.5 1.6 fusion.1
  380.2 12.6 %attend_back_two.1 = (f32[1024,128]{1,0:T(8,128)S(1)}, bf16[2,1024,128]{2,1,0:T(8,128)(2,1)S(1)}, bf16[2,1024,128]{2,1,0:T(8,128)(2,1)S(1)}, f32[1024,128]{1,0:T(8,128)S(1)}) custom-call(s32[9]{0:T(128)S(1)} %pad_add_fusion.1.meta_ref, bf16[6,1024,128]{2,1,0:T(8,128)(2,1)S(1)} %copy-done.16, bf16[6,1024,128]{2,1,0:T(8,128)(2,1)S(1)} %copy-done.17, ...), custom_call_target="tpu_custom_call" | custom-call | flops 40000000000 | bytes 40000000 | tf_op jit(solution)/shard_map/attend_back_two/pallas_call | solution.py:390
  392.8 3.6 collective-permute-start.11
  396.5 4.2 add_convert_fusion.1
  400.7 2.3 fusion.4.down_ref
  403.0 8.3 %collective-permute-done.12 = bf16[384,2048]{1,0:T(8,128)(2,1)S(1)} collective-permute-done((bf16[384,2048]{1,0:T(8,128)(2,1)S(1)}, bf16[384,2048]{1,0:T(8,128)(2,1)S(1)}, u32[]{:S(2)}, u32[]{:S(2)}) %collective-permute-start.12) | collective-permute-done | bytes 1572896 | tf_op jit(solution)/shard_map/ppermute | solution.py:44
  412.3 2.0 fusion
  414.3 136.3 %last.1 = (f32[256,2048]{1,0:T(8,128)}, f32[64,1536]{1,0:T(8,128)}, f32[64,384]{1,0:T(8,128)}, f32[64,384]{1,0:T(8,128)}, f32[64,128]{1,0:T(8,128)}, /*index=5*/...) custom-call(f32[1024,256]{1,0:T(8,128)} %copy-done.18, ...), custom_call_target="tpu_custom_call" | custom-call | flops 60000002048 | bytes 60000000 | tf_op jit(solution)/shard_map/last/pallas_call | solution.py:2051
  550.5 1.5 slice_reduce_fusion
  553.4 3.3 copy.86
  559.5 1.1 copy.91
  560.6 1.1 copy.92
  561.6 1.1 copy.93
  (123 shorter events, 16.3 us)
Async XLA Ops:
  7.0 121.7 %copy-start.3 = (f32[1,128]{1,0:T(1,128)}, f32[1,128]{1,0:T(1,128)S(1)}, u32[]{:S(2)}) copy-start(f32[1,128]{1,0:T(1,128)S(1)} %get-tuple-element.206.query_gain_ref) | copy-start | bytes 1540
  7.0 121.7 %copy-start.4 = (f32[1,128]{1,0:T(1,128)}, f32[1,128]{1,0:T(1,128)S(1)}, u32[]{:S(2)}) copy-start(f32[1,128]{1,0:T(1,128)S(1)} %get-tuple-element.207.key_gain_ref) | copy-start | bytes 1540
  7.9 120.8 %copy-start = (f32[1024,128]{1,0:T(8,128)}, f32[1024,128]{1,0:T(8,128)S(1)}, u32[]{:S(2)}) copy-start(f32[1024,128]{1,0:T(8,128)S(1)} %get-tuple-element.204.cos_ref) | copy-start | bytes 1572868
  7.9 120.8 %copy-start.1 = (f32[1024,128]{1,0:T(8,128)}, f32[1024,128]{1,0:T(8,128)S(1)}, u32[]{:S(2)}) copy-start(f32[1024,128]{1,0:T(8,128)S(1)} %get-tuple-element.205.sin_ref) | copy-start | bytes 1572868
  8.0 124.7 %copy-start.39 = (bf16[256,2048]{1,0:T(8,128)(2,1)S(1)}, bf16[256,2048]{1,0:T(8,128)(2,1)}, u32[]{:S(2)}) copy-start(bf16[256,2048]{1,0:T(8,128)(2,1)} %top_ref.3) | copy-start | bytes 3145732
  128.7 23.7 %copy-start.5 = (bf16[256,2048]{1,0:T(8,128)(2,1)}, bf16[256,2048]{1,0:T(8,128)(2,1)S(1)}, u32[]{:S(2)}) copy-start(bf16[256,2048]{1,0:T(8,128)(2,1)S(1)} %get-tuple-element.114.top_far_ref) | copy-start | bytes 3145732
  128.7 23.7 %copy-start.9 = (bf16[160,2048]{1,0:T(8,128)(2,1)}, bf16[160,2048]{1,0:T(8,128)(2,1)S(1)}, u32[]{:S(2)}) copy-start(bf16[160,2048]{1,0:T(8,128)(2,1)S(1)} %get-tuple-element.124.refs_4_) | copy-start | bytes 1966084
  128.8 24.6 %copy-start.2 = (f32[8,2048]{1,0:T(8,128)}, f32[8,2048]{1,0:T(8,128)S(1)}, u32[]{:S(2)}) copy-start(f32[8,2048]{1,0:T(8,128)S(1)} %get-tuple-element.117.gain_ref) | copy-start | bytes 196612
  128.8 48.3 %collective-permute-start = (bf16[4,128,1280]{2,1,0:T(8,128)(2,1)}, bf16[4,128,1280]{2,1,0:T(8,128)(2,1)}, u32[]{:S(2)}, u32[]{:S(2)}) collective-permute-start(bf16[4,128,1280]{2,1,0:T(8,128)(2,1)} %get-tuple-element.121.refs_1_), channel_id=1, source_target_pairs={{0,2},{1,3},{2,4},{3,5},{4,6},{5,7},{6,0},{7,1},{8,10},{9,11},{10,... | collective-permute-start | bytes 3932168 | tf_op jit(solution)/shard_map/ppermute | solution.py:49
  129.8 43.8 %collective-permute-start.1 = (bf16[160,2048]{1,0:T(8,128)(2,1)S(1)}, bf16[160,2048]{1,0:T(8,128)(2,1)}, u32[]{:S(2)}, u32[]{:S(2)}) collective-permute-start(bf16[160,2048]{1,0:T(8,128)(2,1)S(1)} %get-tuple-element.124.refs_4_), channel_id=1, source_target_pairs={{0,2},{1,3},{2,4},{3,5},{4,6},{5,7},{6,0},{7,1},{8,10},{9,11},{10,... | collective-permute-start | bytes 1966088 | tf_op jit(solution)/shard_map/ppermute | solution.py:49
  132.1 45.0 %collective-permute-start.2 = (bf16[384,2048]{1,0:T(8,128)(2,1)}, bf16[384,2048]{1,0:T(8,128)(2,1)}, u32[]{:S(2)}, u32[]{:S(2)}) collective-permute-start(bf16[384,2048]{1,0:T(8,128)(2,1)} %bitcast.69), channel_id=1, source_target_pairs={{0,16},{8,24},{16,0},{24,8},{1,17},{9,25},{17,1},{25,9},{2,18},{10... | collective-permute-start | bytes 4718600 | tf_op jit(solution)/shard_map/ppermute | solution.py:44
  132.6 40.9 %collective-permute-start.3 = (bf16[256,2048]{1,0:T(8,128)(2,1)S(1)}, bf16[256,2048]{1,0:T(8,128)(2,1)}, u32[]{:S(2)}, u32[]{:S(2)}) collective-permute-start(bf16[256,2048]{1,0:T(8,128)(2,1)S(1)} %copy-done.39), channel_id=1, source_target_pairs={{0,1},{1,0},{2,3},{3,2},{4,5},{5,4},{6,7},{7,6},{8,9},{9,8},{10,11... | collective-permute-start | bytes 3145736 | tf_op jit(solution)/shard_map/ppermute | solution.py:44
  132.6 44.4 %collective-permute-start.4 = (bf16[256,2048]{1,0:T(8,128)(2,1)S(1)}, bf16[256,2048]{1,0:T(8,128)(2,1)}, u32[]{:S(2)}, u32[]{:S(2)}) collective-permute-start(bf16[256,2048]{1,0:T(8,128)(2,1)S(1)} %get-tuple-element.114.top_far_ref), channel_id=1, source_target_pairs={{0,1},{1,0},{2,3},{3,2},{4,5},{5,4},{6,7},{7,6},{8,9},{9,8},{10,11... | collective-permute-start | bytes 3145736 | tf_op jit(solution)/shard_map/ppermute | solution.py:44
  325.9 6.8 %copy-start.13 = (bf16[4,256,384]{2,1,0:T(8,128)(2,1)S(1)}, bf16[4,256,384]{2,1,0:T(8,128)(2,1)}, u32[]{:S(2)}) copy-start(bf16[4,256,384]{2,1,0:T(8,128)(2,1)} %get-tuple-element.130) | copy-start | bytes 2359300
  325.9 6.8 %copy-start.16 = (bf16[6,1024,128]{2,1,0:T(8,128)(2,1)S(1)}, bf16[6,1024,128]{2,1,0:T(8,128)(2,1)}, u32[]{:S(2)}) copy-start(bf16[6,1024,128]{2,1,0:T(8,128)(2,1)} %get-tuple-element.98.query_ref.wide_ref) | copy-start | bytes 4718596
  325.9 26.9 %collective-permute-start.5 = (bf16[160,2048]{1,0:T(8,128)(2,1)}, bf16[160,2048]{1,0:T(8,128)(2,1)}, u32[]{:S(2)}, u32[]{:S(2)}) collective-permute-start(bf16[160,2048]{1,0:T(8,128)(2,1)} %dynamic-slice_bitcast_fusion), channel_id=1, source_target_pairs={{0,2},{1,3},{2,4},{3,5},{4,6},{5,7},{6,0},{7,1},{8,10},{9,11},{10,... | collective-permute-start | bytes 1966088 | tf_op jit(solution)/shard_map/ppermute | solution.py:49
  329.2 49.3 %collective-permute-start.6 = (bf16[4,128,1280]{2,1,0:T(8,128)(2,1)}, bf16[4,128,1280]{2,1,0:T(8,128)(2,1)S(1)}, u32[]{:S(2)}, u32[]{:S(2)}) collective-permute-start(bf16[4,128,1280]{2,1,0:T(8,128)(2,1)} %fusion.2), channel_id=1, source_target_pairs={{0,2},{1,3},{2,4},{3,5},{4,6},{5,7},{6,0},{7,1},{8,10},{9,11},{10,... | collective-permute-start | bytes 3932168 | tf_op jit(solution)/shard_map/ppermute | solution.py:49
  329.2 26.3 %collective-permute-start.7 = (bf16[256,2048]{1,0:T(8,128)(2,1)}, bf16[256,2048]{1,0:T(8,128)(2,1)}, u32[]{:S(2)}, u32[]{:S(2)}) collective-permute-start(bf16[256,2048]{1,0:T(8,128)(2,1)} %get-tuple-element.138), channel_id=1, source_target_pairs={{0,16},{8,24},{16,0},{24,8},{1,17},{9,25},{17,1},{25,9},{2,18},{10... | collective-permute-start | bytes 3145736 | tf_op jit(solution)/shard_map/ppermute | solution.py:44
  330.3 47.7 %collective-permute-start.8 = (bf16[256,2048]{1,0:T(8,128)(2,1)}, bf16[256,2048]{1,0:T(8,128)(2,1)}, u32[]{:S(2)}, u32[]{:S(2)}) collective-permute-start(bf16[256,2048]{1,0:T(8,128)(2,1)} %get-tuple-element.139), channel_id=1, source_target_pairs={{0,1},{1,0},{2,3},{3,2},{4,5},{5,4},{6,7},{7,6},{8,9},{9,8},{10,11... | collective-permute-start | bytes 3145736 | tf_op jit(solution)/shard_map/ppermute | solution.py:44
  331.3 47.2 %collective-permute-start.9 = (bf16[256,2048]{1,0:T(8,128)(2,1)}, bf16[256,2048]{1,0:T(8,128)(2,1)}, u32[]{:S(2)}, u32[]{:S(2)}) collective-permute-start(bf16[256,2048]{1,0:T(8,128)(2,1)} %get-tuple-element.140), channel_id=1, source_target_pairs={{0,17},{1,16},{2,19},{3,18},{4,21},{5,20},{6,23},{7,22},{8,25},{9,... | collective-permute-start | bytes 3145736 | tf_op jit(solution)/shard_map/ppermute | solution.py:2286
  332.7 18.8 %copy-start.25 = (bf16[2,384,2048]{2,1,0:T(8,128)(2,1)S(1)}, bf16[2,384,2048]{2,1,0:T(8,128)(2,1)}, u32[]{:S(2)}) copy-start(bf16[2,384,2048]{2,1,0:T(8,128)(2,1)} %get-tuple-element.154) | copy-start | bytes 9437188
  332.7 18.8 %copy-start.26 = (bf16[2,384,2048]{2,1,0:T(8,128)(2,1)S(1)}, bf16[2,384,2048]{2,1,0:T(8,128)(2,1)}, u32[]{:S(2)}) copy-start(bf16[2,384,2048]{2,1,0:T(8,128)(2,1)} %get-tuple-element.155) | copy-start | bytes 9437188
  352.8 27.4 %copy-start.17 = (bf16[6,1024,128]{2,1,0:T(8,128)(2,1)S(1)}, bf16[6,1024,128]{2,1,0:T(8,128)(2,1)}, u32[]{:S(2)}) copy-start(bf16[6,1024,128]{2,1,0:T(8,128)(2,1)} %get-tuple-element.128.query_ref) | copy-start | bytes 4718596
  352.8 58.5 %collective-permute-start.12 = (bf16[384,2048]{1,0:T(8,128)(2,1)S(1)}, bf16[384,2048]{1,0:T(8,128)(2,1)S(1)}, u32[]{:S(2)}, u32[]{:S(2)}) collective-permute-start(bf16[384,2048]{1,0:T(8,128)(2,1)S(1)} %fusion.3), channel_id=1, source_target_pairs={{0,16},{8,24},{16,0},{24,8},{1,17},{9,25},{17,1},{25,9},{2,18},{10... | collective-permute-start | bytes 4718600 | tf_op jit(solution)/shard_map/ppermute | solution.py:44
  380.1 16.4 %copy-start.28 = (f32[256,2048]{1,0:T(8,128)S(1)}, f32[256,2048]{1,0:T(8,128)}, u32[]{:S(2)}) copy-start(f32[256,2048]{1,0:T(8,128)} %get-tuple-element.126) | copy-start | bytes 6291460
  380.1 32.1 %collective-permute-start.10 = (bf16[4,128,1280]{2,1,0:T(8,128)(2,1)S(1)}, bf16[4,128,1280]{2,1,0:T(8,128)(2,1)}, u32[]{:S(2)}, u32[]{:S(2)}) collective-permute-start(bf16[4,128,1280]{2,1,0:T(8,128)(2,1)S(1)} %fusion.1), channel_id=1, source_target_pairs={{0,2},{1,3},{2,4},{3,5},{4,6},{5,7},{6,0},{7,1},{8,10},{9,11},{10,... | collective-permute-start | bytes 3932168 | tf_op jit(solution)/shard_map/ppermute | solution.py:49
  392.8 7.9 %copy-start.19 = (f32[1024,128]{1,0:T(8,128)}, f32[1024,128]{1,0:T(8,128)S(1)}, u32[]{:S(2)}) copy-start(f32[1024,128]{1,0:T(8,128)S(1)} %get-tuple-element.157.dq_two_ref) | copy-start | bytes 1572868
  392.8 7.9 %copy-start.20 = (bf16[2,1024,128]{2,1,0:T(8,128)(2,1)}, bf16[2,1024,128]{2,1,0:T(8,128)(2,1)S(1)}, u32[]{:S(2)}) copy-start(bf16[2,1024,128]{2,1,0:T(8,128)(2,1)S(1)} %get-tuple-element.159.low_two_ref) | copy-start | bytes 1572868
  392.8 7.9 %copy-start.21 = (bf16[2,1024,128]{2,1,0:T(8,128)(2,1)}, bf16[2,1024,128]{2,1,0:T(8,128)(2,1)S(1)}, u32[]{:S(2)}) copy-start(bf16[2,1024,128]{2,1,0:T(8,128)(2,1)S(1)} %get-tuple-element.160.pair_two_ref) | copy-start | bytes 1572868
  392.8 7.9 %copy-start.22 = (f32[1024,128]{1,0:T(8,128)}, f32[1024,128]{1,0:T(8,128)S(1)}, u32[]{:S(2)}) copy-start(f32[1024,128]{1,0:T(8,128)S(1)} %get-tuple-element.162.own_two_ref) | copy-start | bytes 1572868
  392.8 18.5 %collective-permute-start.11 = (bf16[2,1024,128]{2,1,0:T(8,128)(2,1)S(1)}, bf16[2,1024,128]{2,1,0:T(8,128)(2,1)S(1)}, u32[]{:S(2)}, u32[]{:S(2)}) collective-permute-start(bf16[2,1024,128]{2,1,0:T(8,128)(2,1)S(1)} %get-tuple-element.146), channel_id=1, source_target_pairs={{0,1},{1,0},{2,3},{3,2},{4,5},{5,4},{6,7},{7,6},{8,9},{9,8},{10,11... | collective-permute-start | bytes 1572872 | tf_op jit(solution)/shard_map/ppermute | solution.py:44
  396.5 15.8 %copy-start.27 = (bf16[2,384,2048]{2,1,0:T(8,128)(2,1)S(1)}, bf16[2,384,2048]{2,1,0:T(8,128)(2,1)}, u32[]{:S(2)}) copy-start(bf16[2,384,2048]{2,1,0:T(8,128)(2,1)} %get-tuple-element.155) | copy-start | bytes 9437188
  (22 other events, 69.0 us)
